TPU v7x, 32 devices: a whole 2x2x4 slice. The times are simulated.
32 devices in a mesh: dp: 8 (over z, core), fsdp: 4 (over y, x).
Axes of the slice: x: 2, y: 2, z: 4, core: 2. Of those that a mesh axis runs over, the one named last changes fastest.
Arguments:
- tokens: bfloat16 [32, 320, 1024], P(('dp', 'fsdp')), may hold values from -6 to 6
- cotangent: bfloat16 [32, 320, 1024], P(('dp', 'fsdp')), may hold values from -6 to 6
- counts: int32 [32], P(('dp', 'fsdp')), may hold values from 64 to 320, as said below
- w_qkv: float32 [1024, 3072], P(('dp', 'fsdp')), may hold values from -0.3125 to 0.3125
- w_out: float32 [1024, 1024], P(None, ('dp', 'fsdp')), may hold values from -0.75 to 0.75
- w_up: float32 [1024, 4096], P(('dp', 'fsdp')), may hold values from -0.1875 to 0.1875
- w_down: float32 [4096, 1024], P(None, ('dp', 'fsdp')), may hold values from -0.09375 to 0.09375
- vectors: float32 [12, 1024], P(None, ('dp', 'fsdp')), may hold values from -0.9 to 1.4
- mean_qkv: float32 [1024, 3072], P(('dp', 'fsdp')), may hold values from -28 to 28
- mean_out: float32 [1024, 1024], P(None, ('dp', 'fsdp')), may hold values from -16 to 16
- mean_up: float32 [1024, 4096], P(('dp', 'fsdp')), may hold values from -16 to 16
- mean_down: float32 [4096, 1024], P(None, ('dp', 'fsdp')), may hold values from -32 to 32
- mean_vectors: float32 [12, 1024], P(None, ('dp', 'fsdp')), may hold values from -40 to 40
- square_qkv: float32 [1024, 3072], P(('dp', 'fsdp')), may hold values from 81.92 to 327.68
- square_out: float32 [1024, 1024], P(None, ('dp', 'fsdp')), may hold values from 29.696 to 116.736
- square_up: float32 [1024, 4096], P(('dp', 'fsdp')), may hold values from 29.696 to 116.736
- square_down: float32 [4096, 1024], P(None, ('dp', 'fsdp')), may hold values from 117.76 to 471.04
- square_vectors: float32 [12, 1024], P(None, ('dp', 'fsdp')), may hold values from 204.8 to 819.2
Outputs:
- result: bfloat16 [32, 320, 1024], P(('dp', 'fsdp'))
- token_grad: bfloat16 [32, 320, 1024], P(('dp', 'fsdp'))
- head_peak: float32 [16], replicated
- new_mean_qkv: float32 [1024, 3072], P(('dp', 'fsdp'))
- new_square_qkv: float32 [1024, 3072], P(('dp', 'fsdp'))
- new_w_qkv: float32 [1024, 3072], P(('dp', 'fsdp'))
- new_mean_out: float32 [1024, 1024], P(None, ('dp', 'fsdp'))
- new_square_out: float32 [1024, 1024], P(None, ('dp', 'fsdp'))
- new_w_out: float32 [1024, 1024], P(None, ('dp', 'fsdp'))
- new_mean_up: float32 [1024, 4096], P(('dp', 'fsdp'))
- new_square_up: float32 [1024, 4096], P(('dp', 'fsdp'))
- new_w_up: float32 [1024, 4096], P(('dp', 'fsdp'))
- new_mean_down: float32 [4096, 1024], P(None, ('dp', 'fsdp'))
- new_square_down: float32 [4096, 1024], P(None, ('dp', 'fsdp'))
- new_w_down: float32 [4096, 1024], P(None, ('dp', 'fsdp'))
- new_mean_vectors: float32 [12, 1024], P(None, ('dp', 'fsdp'))
- new_square_vectors: float32 [12, 1024], P(None, ('dp', 'fsdp'))
- new_vectors: float32 [12, 1024], P(None, ('dp', 'fsdp'))
Inputs may be any that keep to these rules, and one draw needn't show every extreme that they name: `counts`: in every draw some sequence keeps all 320 slots.
All inputs are finite; a program needn't handle non-finite values.
Results may differ from a plain program's by a relative error of at most 0.012.
The roundings to bfloat16 on the way count: a program that leaves them out, or rounds other values in their place, can miss the bound.
Values may be sent and summed in bfloat16 or wider, within the bound.
No kernel may reach another device: no remote copies, remote signals or barrier semaphores. Data moves between devices by JAX's collectives and lax.ppermute only.
A program may use at most 192 MiB of HBM per device.

v0:
```python
from functools import partial

import jax
import jax.numpy as jnp
from jax import lax
from jax.sharding import PartitionSpec as P

H = 16
STEP = 10


beta_one = 0.9
beta_two = 0.95
adam_epsilon = 1e-08
weight_decay = 0.1
matrix_rate = 0.1
vector_rate = 0.5
clip_limit = 8.0
norm_epsilon = 1e-06
masked_value = -1e30


def layer_norm(values, gain_row, shift_row):
    centered = values - jnp.mean(values, -1, keepdims=True)
    spread = jnp.mean(centered * centered, -1, keepdims=True)
    return centered * lax.rsqrt(spread + norm_epsilon) * gain_row + shift_row


def contract_rows(first_op, second_op):
    return lax.dot_general(
        first_op, second_op, (((0,), (0,)), ((), ())), preferred_element_type=jnp.float32
    )


def contract_cols(first_op, second_op):
    return lax.dot_general(
        first_op, second_op, (((1,), (1,)), ((), ())), preferred_element_type=jnp.float32
    )


def adam_step(weight, gradient, mean_old, square_old, step_rate, decay_rate):
    mean_new = beta_one * mean_old + (1.0 - beta_one) * gradient
    square_new = beta_two * square_old + (1.0 - beta_two) * gradient * gradient
    fix_one = 1.0 - beta_one**STEP
    fix_two = 1.0 - beta_two**STEP
    stepped = weight - step_rate * (
        mean_new / fix_one / (jnp.sqrt(square_new / fix_two) + adam_epsilon) + decay_rate * weight
    )
    return (mean_new, square_new, stepped)


def local(
    tokens,
    cotangent,
    counts,
    w_qkv,
    w_out,
    w_up,
    w_down,
    vectors,
    mean_qkv,
    mean_out,
    mean_up,
    mean_down,
    mean_vectors,
    square_qkv,
    square_out,
    square_up,
    square_down,
    square_vectors,
):
    seq_count, slot_count, model_width = tokens.shape
    row_count = seq_count * slot_count
    head_width = model_width // H
    score_scale = head_width ** (-0.5)
    shard_qkv = w_qkv.astype(jnp.bfloat16)
    shard_out = w_out.astype(jnp.bfloat16)
    shard_up = w_up.astype(jnp.bfloat16)
    shard_down = w_down.astype(jnp.bfloat16)
    shard_vectors = vectors.astype(jnp.bfloat16)
    low_qkv, low_out, low_up, low_down, low_vectors = (
        lax.all_gather(shard_qkv, ("dp", "fsdp"), axis=0, tiled=True),
        lax.all_gather(shard_out, ("dp", "fsdp"), axis=1, tiled=True),
        lax.all_gather(shard_up, ("dp", "fsdp"), axis=0, tiled=True),
        lax.all_gather(shard_down, ("dp", "fsdp"), axis=1, tiled=True),
        lax.all_gather(shard_vectors, ("dp", "fsdp"), axis=1, tiled=True),
    )
    vector_rows = low_vectors.astype(jnp.float32)
    keep_mask = (
        lax.broadcasted_iota(jnp.int32, (seq_count, slot_count), 1) < counts[:, None]
    ).astype(jnp.float32)
    keep_rows = keep_mask.reshape(row_count, 1)
    valid_key = keep_mask[:, None, None, :] > 0.5
    valid_pair = valid_key & (keep_mask[:, None, :, None] > 0.5)
    inputs = tokens.astype(jnp.float32).reshape(row_count, model_width)
    head_shape = (seq_count, slot_count, H, head_width)
    normed, norm_back_one = jax.vjp(layer_norm, inputs, vector_rows[0], vector_rows[1])
    normed_low = normed.astype(jnp.bfloat16)
    projected = jnp.dot(normed_low, low_qkv, preferred_element_type=jnp.float32)
    queries = (projected[:, :model_width] + vector_rows[4]).astype(jnp.bfloat16).reshape(head_shape)
    key_part = projected[:, model_width : 2 * model_width].astype(jnp.bfloat16).reshape(head_shape)
    values_part = (
        (projected[:, 2 * model_width :] + vector_rows[5]).astype(jnp.bfloat16).reshape(head_shape)
    )
    raw_scores = (
        jnp.einsum("sqhc,skhc->shqk", queries, key_part, preferred_element_type=jnp.float32)
        * score_scale
    )
    local_peak = jnp.max(jnp.where(valid_pair, raw_scores, masked_value), axis=(0, 2, 3))
    scores = jnp.where(valid_key, raw_scores, masked_value)
    row_top = jnp.max(scores, -1, keepdims=True)
    exponent = jnp.exp(scores - row_top)
    row_total = jnp.sum(exponent, -1, keepdims=True)
    log_total = row_top + jnp.log(row_total)
    probs_low = (exponent / row_total).astype(jnp.bfloat16)
    attended = jnp.einsum(
        "shqk,skhc->sqhc", probs_low, values_part, preferred_element_type=jnp.float32
    )
    attended = attended.reshape(row_count, model_width).astype(jnp.bfloat16)
    middle = (
        inputs + jnp.dot(attended, low_out, preferred_element_type=jnp.float32) + vector_rows[6]
    )
    normed_two, norm_back_two = jax.vjp(layer_norm, middle, vector_rows[2], vector_rows[3])
    normed_two_low = normed_two.astype(jnp.bfloat16)
    bias_up = vector_rows[8:].reshape(-1)
    hidden_pre = jnp.dot(normed_two_low, low_up, preferred_element_type=jnp.float32) + bias_up
    hidden, gelu_back = jax.vjp(partial(jax.nn.gelu, approximate=False), hidden_pre)
    hidden_low = hidden.astype(jnp.bfloat16)
    result = keep_rows * (
        middle + jnp.dot(hidden_low, low_down, preferred_element_type=jnp.float32) + vector_rows[7]
    )
    result_out = result.astype(jnp.bfloat16).reshape(seq_count, slot_count, model_width)
    head_peak = lax.pmax(local_peak, ("dp", "fsdp"))
    back_qkv, back_out, back_up, back_down = (
        lax.all_gather(shard_qkv, ("dp", "fsdp"), axis=0, tiled=True),
        lax.all_gather(shard_out, ("dp", "fsdp"), axis=1, tiled=True),
        lax.all_gather(shard_up, ("dp", "fsdp"), axis=0, tiled=True),
        lax.all_gather(shard_down, ("dp", "fsdp"), axis=1, tiled=True),
    )
    d_result = keep_rows * cotangent.astype(jnp.float32).reshape(row_count, model_width)
    d_down_low = d_result.astype(jnp.bfloat16)
    grad_bias_down = jnp.sum(d_down_low.astype(jnp.float32), 0)
    d_hidden = contract_cols(d_down_low, back_down)
    d_pre_low = gelu_back(d_hidden)[0].astype(jnp.bfloat16)
    grad_bias_up = jnp.sum(d_pre_low.astype(jnp.float32), 0)
    d_normed_two = contract_cols(d_pre_low, back_up)
    d_middle_part, grad_gain_two, grad_shift_two = norm_back_two(d_normed_two)
    d_middle = d_result + d_middle_part
    d_branch_low = d_middle.astype(jnp.bfloat16)
    grad_bias_out = jnp.sum(d_branch_low.astype(jnp.float32), 0)
    d_attended = contract_cols(d_branch_low, back_out).astype(jnp.bfloat16).reshape(head_shape)
    raw_again = (
        jnp.einsum("sqhc,skhc->shqk", queries, key_part, preferred_element_type=jnp.float32)
        * score_scale
    )
    attention_probs = jnp.exp(jnp.where(valid_key, raw_again, masked_value) - log_total)
    probs_again_low = attention_probs.astype(jnp.bfloat16)
    d_probs = jnp.einsum(
        "sqhc,skhc->shqk", d_attended, values_part, preferred_element_type=jnp.float32
    )
    d_values = jnp.einsum(
        "shqk,sqhc->skhc", probs_again_low, d_attended, preferred_element_type=jnp.float32
    ).astype(jnp.bfloat16)
    d_scores = (
        attention_probs * (d_probs - jnp.sum(attention_probs * d_probs, -1, keepdims=True))
    ).astype(jnp.bfloat16)
    d_queries = (
        jnp.einsum("shqk,skhc->sqhc", d_scores, key_part, preferred_element_type=jnp.float32)
        * score_scale
    ).astype(jnp.bfloat16)
    d_keys = (
        jnp.einsum("shqk,sqhc->skhc", d_scores, queries, preferred_element_type=jnp.float32)
        * score_scale
    ).astype(jnp.bfloat16)
    d_queries = d_queries.reshape(row_count, model_width)
    d_keys = d_keys.reshape(row_count, model_width)
    d_values = d_values.reshape(row_count, model_width)
    d_projected = jnp.concatenate([d_queries, d_keys, d_values], 1)
    grad_bias_query = jnp.sum(d_queries.astype(jnp.float32), 0)
    grad_bias_value = jnp.sum(d_values.astype(jnp.float32), 0)
    d_normed = contract_cols(d_projected, back_qkv)
    d_inputs_part, grad_gain_one, grad_shift_one = norm_back_one(d_normed)
    token_grad = (
        (d_middle + d_inputs_part).astype(jnp.bfloat16).reshape(seq_count, slot_count, model_width)
    )
    vector_grads = jnp.concatenate(
        [
            jnp.stack(
                [
                    grad_gain_one,
                    grad_shift_one,
                    grad_gain_two,
                    grad_shift_two,
                    grad_bias_query,
                    grad_bias_value,
                    grad_bias_out,
                    grad_bias_down,
                ],
                0,
            ),
            grad_bias_up.reshape(-1, model_width),
        ],
        0,
    )
    vector_grads_turned = vector_grads.T
    row_sums = lax.psum_scatter(
        jnp.concatenate(
            [contract_rows(normed_low, d_projected), contract_rows(normed_two_low, d_pre_low)], 1
        ),
        ("dp", "fsdp"),
        scatter_dimension=0,
        tiled=True,
    )
    column_sums = lax.psum_scatter(
        jnp.concatenate(
            [
                contract_rows(d_branch_low, attended),
                contract_rows(d_down_low, hidden_low),
                vector_grads_turned,
            ],
            1,
        ),
        ("dp", "fsdp"),
        scatter_dimension=0,
        tiled=True,
    )
    reduced_qkv = row_sums[:, : 3 * model_width]
    reduced_up = row_sums[:, 3 * model_width :]
    reduced_out = column_sums[:, :model_width].T
    reduced_down = column_sums[:, model_width : model_width + w_down.shape[0]].T
    reduced_vectors = column_sums[:, model_width + w_down.shape[0] :].T
    mean_q, square_q, stepped_qkv = adam_step(
        w_qkv, reduced_qkv, mean_qkv, square_qkv, matrix_rate, weight_decay
    )
    mean_o, square_o, new_out = adam_step(
        w_out, reduced_out, mean_out, square_out, matrix_rate, weight_decay
    )
    mean_u, square_u, new_up = adam_step(
        w_up, reduced_up, mean_up, square_up, matrix_rate, weight_decay
    )
    mean_d, square_d, new_down = adam_step(
        w_down, reduced_down, mean_down, square_down, matrix_rate, weight_decay
    )
    mean_v, square_v, stepped_vectors = adam_step(
        vectors, reduced_vectors, mean_vectors, square_vectors, vector_rate, 0.0
    )
    shrink = jnp.sqrt(clip_limit / jnp.maximum(head_peak, clip_limit))
    head_cols = jnp.repeat(shrink, head_width)
    qkv_scale = jnp.concatenate([head_cols, head_cols, jnp.ones((model_width,), jnp.float32)])
    new_qkv = stepped_qkv * qkv_scale[None, :]
    col_count = vectors.shape[1]
    first_col = lax.axis_index(("dp", "fsdp")) * col_count
    col_head = (first_col + jnp.arange(col_count, dtype=jnp.int32)) // head_width
    col_shrink = jnp.sum(
        jnp.where(
            col_head[:, None] == jnp.arange(H, dtype=jnp.int32)[None, :], shrink[None, :], 0.0
        ),
        1,
    )
    row_pick = (jnp.arange(vectors.shape[0], dtype=jnp.int32) == 4)[:, None]
    new_vectors = jnp.where(row_pick, stepped_vectors * col_shrink[None, :], stepped_vectors)
    return (
        result_out,
        token_grad,
        head_peak,
        mean_q,
        square_q,
        new_qkv,
        mean_o,
        square_o,
        new_out,
        mean_u,
        square_u,
        new_up,
        mean_d,
        square_d,
        new_down,
        mean_v,
        square_v,
        new_vectors,
    )


def solution(mesh):
    return jax.shard_map(
        local,
        mesh=mesh,
        in_specs=(
            P(("dp", "fsdp"), None, None),
            P(("dp", "fsdp"), None, None),
            P(("dp", "fsdp")),
            P(("dp", "fsdp"), None),
            P(None, ("dp", "fsdp")),
            P(("dp", "fsdp"), None),
            P(None, ("dp", "fsdp")),
            P(None, ("dp", "fsdp")),
            P(("dp", "fsdp"), None),
            P(None, ("dp", "fsdp")),
            P(("dp", "fsdp"), None),
            P(None, ("dp", "fsdp")),
            P(None, ("dp", "fsdp")),
            P(("dp", "fsdp"), None),
            P(None, ("dp", "fsdp")),
            P(("dp", "fsdp"), None),
            P(None, ("dp", "fsdp")),
            P(None, ("dp", "fsdp")),
        ),
        out_specs=(
            P(("dp", "fsdp"), None, None),
            P(("dp", "fsdp"), None, None),
            P(),
            P(("dp", "fsdp"), None),
            P(("dp", "fsdp"), None),
            P(("dp", "fsdp"), None),
            P(None, ("dp", "fsdp")),
            P(None, ("dp", "fsdp")),
            P(None, ("dp", "fsdp")),
            P(("dp", "fsdp"), None),
            P(("dp", "fsdp"), None),
            P(("dp", "fsdp"), None),
            P(None, ("dp", "fsdp")),
            P(None, ("dp", "fsdp")),
            P(None, ("dp", "fsdp")),
            P(None, ("dp", "fsdp")),
            P(None, ("dp", "fsdp")),
            P(None, ("dp", "fsdp")),
        ),
        check_vma=False,
    )
```

profile of v0, /device:TPU:0, one launch (start us, length us, event | category | flops | bytes accessed | tf_op | source)
XLA Modules:
  0.0 1456.0 jit_solution(8651416785991982454)
XLA Ops:
  7.2 1.8 convert_element_type.149
  9.1 1.5 convert_element_type.157
  10.7 1.8 convert_element_type.159
  12.5 1.8 convert_element_type.161
  15.1 71.4 %all-gather = bf16[32,32,12]{1,2,0:T(8,128)(2,1)S(1)} all-gather(bf16[1,32,12]{1,2,0:T(8,128)(2,1)S(1)} %convert_bitcast_fusion.1), channel_id=1, replica_groups=mesh['dp'=8,'fsdp'=4] {'dp','fsdp'}, dimensions={0}, use_global_device_ids=true | all-gather | bytes 25344 | tf_op jit(solution)/shard_map/all_gather | solution.py:86
  87.4 1.3 convert_reduce_fusion.1
  89.8 5.1 fusion.59
  94.9 0.9 slice.113
  96.9 1.7 copy.121
  98.7 2.2 fusion.63
  100.9 4.2 select_reduce_fusion
  105.0 2.2 fusion.21
  107.3 36.0 %all-gather.8.cloned.1.call-done = bf16[1024,1024]{0,1:T(8,128)(2,1)} async-done(((bf16[1024,32]{0,1:T(8,128)(2,1)}), bf16[1024,1024]{0,1:T(8,128)(2,1)}) %all-gather.8.cloned.1.call-update) | async-done | bytes 2097168 | tf_op jit(solution)/shard_map/all_gather | solution.py:83
  143.3 2.7 fusion.74
  146.4 76.8 %all-gather.10.cloned.1.call-done = bf16[1024,4096]{1,0:T(8,128)(2,1)} async-done(((bf16[32,4096]{1,0:T(8,128)(2,1)}), bf16[1024,4096]{1,0:T(8,128)(2,1)}) %all-gather.10.cloned.1.call-update) | async-done | bytes 8388624 | tf_op jit(solution)/shard_map/all_gather | solution.py:84
  223.2 17.8 %multiply_convert_fusion.1 = (bf16[320,4096]{1,0:T(8,128)(2,1)}, f32[320,4096]{1,0:T(8,128)}, f32[320,4096]{1,0:T(8,128)}) fusion(f32[4096]{0:T(1024)S(1)} %bitcast.199, bf16[1024,4096]{1,0:T(8,128)(2,1)} %all-gather.10.cloned.1.call-done, f32[320,1024]{1,0:T(8,128)S(1)} %get-tuple-element.152, f32[1024]{0:T(1024)S(1)} %bitcast.192, ...), kind=kOutput, calls=%fused_computation.16 | convolution fusion | flops 2772500480 | bytes 22833664 | tf_op jit(solution)/shard_map/dot_general | solution.py:126
  241.0 61.7 %all-gather.12.cloned.1.call-done = bf16[4096,1024]{0,1:T(8,128)(2,1)} async-done(((bf16[4096,32]{0,1:T(8,128)(2,1)}), bf16[4096,1024]{0,1:T(8,128)(2,1)}) %all-gather.12.cloned.1.call-update) | async-done | bytes 8388624 | tf_op jit(solution)/shard_map/all_gather | solution.py:85
  302.7 10.6 convert_reduce_fusion
  313.3 3.2 multiply_reduce_fusion.1
  318.3 1.7 convolution_convert_fusion
  319.9 2.2 copy.123
  322.2 5.7 convert_reduce_fusion.2
  327.9 5.6 multiply_reduce_fusion
  333.5 2.7 multiply_convert_fusion
  336.3 1.3 multiply_convert_fusion.2
  337.6 0.9 convert_reduce_fusion.3
  338.6 3.3 fusion.75
  341.9 4.0 fusion.64
  346.1 2.0 fusion.30
  348.1 1.0 copy.127
  349.1 6.7 fusion.52
  355.9 7.5 pad_maximum_fusion.1
  363.7 5.4 fusion.38
  369.1 6.5 fusion.62
  375.6 9.9 pad_maximum_fusion
  388.2 42.2 %pmax.7 = f32[16]{0:T(128)S(1)} all-reduce(f32[16]{0:T(128)S(1)} %copy-done.34), channel_id=1, replica_groups=mesh['dp'=8,'fsdp'=4] {'dp','fsdp'}, use_global_device_ids=true, to_apply=%region_12.13 | all-reduce | flops 16 | bytes 128 | tf_op jit(solution)/shard_map/pmax | solution.py:133
  432.2 3.0 fusion.41
  435.2 8.0 fusion.37
  443.3 376.4 %reduce-scatter.5.cloned.1.call-done = f32[32,5132]{1,0:T(8,128)} async-done(((f32[1024,5132]{1,0:T(8,128)}), f32[32,5132]{1,0:T(8,128)}) %reduce-scatter.5.cloned.1.call-update) | async-done | bytes 656912 | tf_op jit(solution)/shard_map/reduce_scatter | solution.py:214
  819.7 1.5 multiply_select_fusion.1
  821.2 1.4 copy.133
  822.6 1.4 copy.134
  824.0 1.4 copy.135
  825.4 1.8 multiply_subtract_fusion.2
  827.2 2.4 multiply_subtract_fusion
  829.7 614.1 %reduce-scatter.3.cloned.1.call-done = f32[32,7168]{1,0:T(8,128)} async-done(((f32[1024,7168]{1,0:T(8,128)}), f32[32,7168]{1,0:T(8,128)}) %reduce-scatter.3.cloned.1.call-update) | async-done | bytes 917520 | tf_op jit(solution)/shard_map/reduce_scatter | solution.py:206
  1443.8 2.6 multiply_subtract_fusion.1
  1446.4 2.3 subtract_multiply_fusion
  (139 shorter events, 10.5 us)
Async XLA Ops:
  7.2 81.5 %copy-start.2 = (bf16[1,320,1024]{2,1,0:T(8,128)(2,1)S(1)}, bf16[1,320,1024]{2,1,0:T(8,128)(2,1)}, u32[]{:S(2)}) copy-start(bf16[1,320,1024]{2,1,0:T(8,128)(2,1)} %param.18) | copy-start | bytes 1966084
  7.2 82.6 %all-gather.6.cloned.1.call-start = ((), (), s32[]{:S(2)}) async-start(), calls=%async_computation.2 | async-start | bytes 6488064 | tf_op jit(solution)/shard_map/all_gather | solution.py:82
  9.0 134.3 %all-gather.8.cloned.1.call-start = ((), (), s32[]{:S(2)}) async-start(), calls=%async_computation.3 | async-start | bytes 2162688 | tf_op jit(solution)/shard_map/all_gather | solution.py:83
  10.6 212.6 %all-gather.10.cloned.1.call-start = ((), (), s32[]{:S(2)}) async-start(), calls=%async_computation.4 | async-start | bytes 8650752 | tf_op jit(solution)/shard_map/all_gather | solution.py:84
  12.5 290.2 %all-gather.12.cloned.1.call-start = ((), (), s32[]{:S(2)}) async-start(), calls=%async_computation.5 | async-start | bytes 8650752 | tf_op jit(solution)/shard_map/all_gather | solution.py:85
  14.3 805.4 %reduce-scatter.5.cloned.1.call-start = ((), (), s32[]{:S(2)}) async-start(), calls=%async_computation.7 | async-start | bytes 22167552 | tf_op jit(solution)/shard_map/reduce_scatter | solution.py:214
  96.5 8.5 copy-start.11
  96.9 3.9 copy-start.5
  98.6 2.2 copy-start.3
  100.8 4.2 copy-start
  107.3 39.1 %copy-start.22 = (bf16[16,64,320]{2,1,0:T(8,128)(2,1)}, bf16[16,64,320]{2,1,0:T(8,128)(2,1)S(1)}, u32[]{:S(2)}) copy-start(bf16[16,64,320]{2,1,0:T(8,128)(2,1)S(1)} %fusion.21) | copy-start | bytes 1966084
  223.2 79.5 %copy-start.7 = (bf16[1,320,1024]{2,1,0:T(8,128)(2,1)S(1)}, bf16[1,320,1024]{2,1,0:T(8,128)(2,1)}, u32[]{:S(2)}) copy-start(bf16[1,320,1024]{2,1,0:T(8,128)(2,1)} %param.19) | copy-start | bytes 1966084
  302.7 10.6 copy-start.35
  313.3 3.3 copy-start.16
  313.3 3.8 copy-start.8
  316.5 1.7 copy-start.36
  317.4 0.8 copy-start.9
  322.2 5.7 copy-start.12
  322.2 5.7 copy-start.13
  322.2 11.3 slice-start
  327.9 14.0 copy-start.21
  327.9 5.6 slice-start.1
  333.5 2.7 copy-start.6
  336.2 1.4 copy-start.4
  336.3 2.3 copy-start.10
  336.3 2.3 copy-start.23
  337.6 4.2 copy-start.14
  337.6 4.2 slice-start.2
  338.6 7.3 copy-start.15
  338.6 3.3 slice-start.3
  349.1 6.8 copy-start.1
  349.1 6.8 copy-start.17
  363.4 1080.3 %reduce-scatter.3.cloned.1.call-start = ((), (), s32[]{:S(2)}) async-start(), calls=%async_computation.6 | async-start | bytes 30277632 | tf_op jit(solution)/shard_map/reduce_scatter | solution.py:206
  385.5 0.7 copy-start.30
  385.5 0.8 copy-start.31
  385.5 1.5 copy-start.32
  385.5 2.7 copy-start.34
  386.2 49.0 %copy-start.33 = (f32[1,1024]{1,0:T(1,128)S(1)}, f32[1,1024]{1,0:T(1,128)}, u32[]{:S(2)}) copy-start(f32[1,1024]{1,0:T(1,128)} %get-tuple-element.141) | copy-start | bytes 12292
  430.4 0.5 copy-start.37
  435.2 390.2 %copy-start.27 = (f32[1024,32]{0,1:T(8,128)S(1)}, f32[1024,32]{0,1:T(8,128)}, u32[]{:S(2)}) copy-start(f32[1024,32]{0,1:T(8,128)} %param.22) | copy-start | bytes 393220
  435.2 392.0 %copy-start.18 = (f32[4096,32]{0,1:T(8,128)S(1)}, f32[4096,32]{0,1:T(8,128)}, u32[]{:S(2)}) copy-start(f32[4096,32]{0,1:T(8,128)} %param.24) | copy-start | bytes 1572868
  435.2 392.0 %copy-start.24 = (f32[4096,32]{0,1:T(8,128)S(1)}, f32[4096,32]{0,1:T(8,128)}, u32[]{:S(2)}) copy-start(f32[4096,32]{0,1:T(8,128)} %param.34) | copy-start | bytes 1572868
  435.2 392.0 %copy-start.25 = (f32[4096,32]{0,1:T(8,128)S(1)}, f32[4096,32]{0,1:T(8,128)}, u32[]{:S(2)}) copy-start(f32[4096,32]{0,1:T(8,128)} %param.29) | copy-start | bytes 1572868
  443.3 1000.5 %copy-start.19 = (f32[32,4096]{1,0:T(8,128)S(1)}, f32[32,4096]{1,0:T(8,128)}, u32[]{:S(2)}) copy-start(f32[32,4096]{1,0:T(8,128)} %param.23) | copy-start | bytes 1572868
  443.3 1000.5 %copy-start.26 = (f32[32,4096]{1,0:T(8,128)S(1)}, f32[32,4096]{1,0:T(8,128)}, u32[]{:S(2)}) copy-start(f32[32,4096]{1,0:T(8,128)} %param.33) | copy-start | bytes 1572868
  443.3 1003.1 %copy-start.20 = (f32[32,3072]{1,0:T(8,128)S(1)}, f32[32,3072]{1,0:T(8,128)}, u32[]{:S(2)}) copy-start(f32[32,3072]{1,0:T(8,128)} %param.21) | copy-start | bytes 1179652
  443.3 1003.1 %copy-start.28 = (f32[32,3072]{1,0:T(8,128)S(1)}, f32[32,3072]{1,0:T(8,128)}, u32[]{:S(2)}) copy-start(f32[32,3072]{1,0:T(8,128)} %param.31) | copy-start | bytes 1179652
  821.2 625.2 %copy-start.29 = (f32[3072]{0:T(1024)S(1)}, f32[3072]{0:T(1024)}, u32[]{:S(2)}) copy-start(f32[3072]{0:T(1024)} %pad_maximum_fusion.5) | copy-start | bytes 36868
Sparse Core Ops, SparseCore 0:
  11.5 73.0 all-gather.5
  88.1 55.1 all-gather.7
  146.8 76.3 all-gather.9
  226.5 76.1 all-gather.11
  363.6 456.1 reduce-scatter.4
  822.0 621.7 reduce-scatter.2
where the time goes:
time: 1460 us
  waiting for transfers between devices  1170 us (80%)
  blocking collectives  114 us (8%)
  matrix products  92.8 us (6%)
  other arithmetic  52.4 us (4%)
  between operations  15.8 us (1%)
  local copies, waits for them, and re-layouts  15.5 us (1%)
    reduce_scatter x1, waiting for transfers between devices, local(): lax.psum_scatter(jnp.concatenate([contract_rows(normed_low, d_projected),...  614 us
    reduce_scatter x1, waiting for transfers between devices, local(): lax.psum_scatter(jnp.concatenate([contract_rows(d_branch_low, attended),...  376 us
    all_gather x1, waiting for transfers between devices, local(): lax.all_gather(shard_up, ('dp', 'fsdp'), axis=0, tiled=True)  76.8 us
    all_gather x1, blocking collectives, local(): lax.all_gather(shard_vectors, ('dp', 'fsdp'), axis=1, tiled=True)  71.4 us
    all_gather x1, waiting for transfers between devices, local(): lax.all_gather(shard_down, ('dp', 'fsdp'), axis=1, tiled=True)  61.7 us
    pmax x1, blocking collectives, local(): head_peak = lax.pmax(local_peak, ('dp', 'fsdp'))  42.2 us
    all_gather x1, waiting for transfers between devices, local(): lax.all_gather(shard_out, ('dp', 'fsdp'), axis=1, tiled=True)  36 us
  transfers between devices with their start and end apart: 6, of which 5 were waited for; matrix products, arithmetic and copies ran while one was open for 6% of the time, Pallas kernels for 0%

commit v1 on v0

v1 whole, which is shorter than its diff:
```python
from functools import partial

import jax
import jax.numpy as jnp
import numpy as np
from jax import lax
from jax.experimental import pallas as pl
from jax.experimental.pallas import tpu as pltpu
from jax.sharding import PartitionSpec as P

H = 16
STEP = 10


beta_one = 0.9
beta_two = 0.95
adam_epsilon = 1e-08
weight_decay = 0.1
matrix_rate = 0.1
vector_rate = 0.5
clip_limit = 8.0
norm_epsilon = 1e-06
masked_value = -1e30
TILE = 512
PAIR = 128
HALF_ROOT = 0.5**0.5
DENSITY = 0.3989422804014327
F32 = jnp.float32
BF16 = jnp.bfloat16


def adam_step(weight, gradient, mean_old, square_old, step_rate, decay_rate):
    mean_new = beta_one * mean_old + (1.0 - beta_one) * gradient
    square_new = beta_two * square_old + (1.0 - beta_two) * gradient * gradient
    fix_one = 1.0 - beta_one**STEP
    fix_two = 1.0 - beta_two**STEP
    stepped = weight - step_rate * (
        mean_new / fix_one / (jnp.sqrt(square_new / fix_two) + adam_epsilon) + decay_rate * weight
    )
    return (mean_new, square_new, stepped)


def bit_names(letter, count):
    return tuple(letter + str(at) for at in range(count))


class Links:
    def __init__(self, dp_count, inner_count):
        self.device_count = dp_count * inner_count
        inner_bits = inner_count.bit_length() - 1
        z_bits = bit_names("z", dp_count.bit_length() - 2)
        x_bits = bit_names("x", inner_bits // 2)
        y_bits = bit_names("y", inner_bits - inner_bits // 2)
        self.place = {"c": ("dp", dp_count, 0)}
        self.place.update({bit: ("dp", dp_count, at + 1) for at, bit in enumerate(z_bits)})
        self.place.update({bit: ("fsdp", inner_count, at) for at, bit in enumerate(x_bits)})
        self.place.update(
            {bit: ("fsdp", inner_count, at + len(x_bits)) for at, bit in enumerate(y_bits)}
        )
        self.bits = ("c",) + y_bits + x_bits + z_bits
        self.orders = (y_bits + x_bits, x_bits + y_bits)
        self.z_bits = z_bits
        self.y_bits = y_bits
        self.inner_bits = inner_bits

    def true_block(self):
        masks = []
        for block in range(self.device_count):
            mask = 0
            for at, bit in enumerate(reversed(self.bits)):
                if block >> at & 1:
                    axis, _, place = self.place[bit]
                    mask |= 1 << (place + (self.inner_bits if axis == "dp" else 0))
            masks.append(mask)
        return lax.axis_index(("dp", "fsdp")) ^ jnp.array(masks, jnp.int32)

    def exchange(self, values, bit):
        axis, count, place = self.place[bit]
        return lax.ppermute(values, axis, [(at, at ^ (1 << place)) for at in range(count)])


class Order:
    def __init__(self):
        self.ended = ()

    def __call__(self, call, *operands):
        operands, _ = lax.optimization_barrier((operands, self.ended))
        result = call(*operands)
        self.ended = result
        return result

    def settle(self, value):
        return self(lambda come: come, value)


def run(body, operands, outs, grid=(), in_specs=None, out_specs=None, scratch=()):
    whole = pl.BlockSpec(memory_space=pltpu.VMEM)
    return pl.pallas_call(
        body,
        out_shape=[jax.ShapeDtypeStruct(shape, kind) for shape, kind in outs],
        grid=grid,
        in_specs=in_specs or [whole] * len(operands),
        out_specs=out_specs or [whole] * len(outs),
        scratch_shapes=scratch,
        compiler_params=pltpu.CompilerParams(vmem_limit_bytes=12 * 2**20),
        cost_estimate=pl.CostEstimate(flops=30 * 10**9, bytes_accessed=1000, transcendentals=0),
    )(*operands)


def fixed(shape):
    return pl.BlockSpec(shape, lambda j: (0,) * len(shape))


def mm(first, second):
    return lax.dot_general(first, second, (((1,), (0,)), ((), ())), preferred_element_type=F32)


def mm_turned(first, second):
    return lax.dot_general(first, second, (((1,), (1,)), ((), ())), preferred_element_type=F32)


def mm_rows(first, second):
    return lax.dot_general(first, second, (((0,), (0,)), ((), ())), preferred_element_type=F32)


def pieces(values, count=3):
    out = []
    for _ in range(count):
        piece = values.astype(BF16)
        out.append(piece)
        values = values - piece.astype(F32)
    return out


def normalized(values):
    centered = values - jnp.mean(values, -1, keepdims=True)
    scale = lax.rsqrt(jnp.mean(centered * centered, -1, keepdims=True) + norm_epsilon)
    return centered * scale, scale


def norm_back(grad, values, gain):
    unit, scale = normalized(values)
    inner = grad * gain
    d_values = scale * (
        inner
        - jnp.mean(inner, -1, keepdims=True)
        - unit * jnp.mean(inner * unit, -1, keepdims=True)
    )
    return (
        d_values,
        jnp.sum(grad * unit, 0, keepdims=True),
        jnp.sum(grad, 0, keepdims=True),
    )


def first_norm(inputs, mine, other, to_relative):
    rows, width = inputs.shape
    half = width // 2

    def body(
        x_ref, mine_ref, other_ref, turn_ref, low_ref, high_ref, lowt_ref, hight_ref, rel_ref, true_ref
    ):
        turned = jnp.concatenate(
            [mine_ref[...].astype(F32).T, other_ref[...].astype(F32).T], 1
        )[:16]
        rel_ref[...] = turned
        true_ref[...] = mm_turned(turned.astype(BF16), turn_ref[...])
        unit, _ = normalized(x_ref[...].astype(F32))
        normed = (unit * turned[0:1] + turned[1:2]).astype(BF16)
        low_ref[...] = normed[:, :half]
        high_ref[...] = normed[:, half:]
        lowt_ref[...] = normed[:, :half].T
        hight_ref[...] = normed[:, half:].T

    vectors_at = mine.shape[1] // PAIR - 1
    weights = pl.BlockSpec((half, PAIR), lambda j: (0, vectors_at))
    return run(
        body,
        (inputs, mine, other, to_relative),
        [((rows, half), BF16)] * 2 + [((half, rows), BF16)] * 2 + [((16, width), F32)] * 2,
        (1,),
        [fixed(inputs.shape), weights, weights, fixed(to_relative.shape)],
        [fixed((rows, half))] * 2 + [fixed((half, rows))] * 2 + [fixed((16, width))] * 2,
    )


def project(at, low, high, mine, other, true_vectors):
    rows, half = low.shape

    def body(low_ref, high_ref, mine_ref, other_ref, vec_ref, out_ref):
        j = pl.program_id(0)
        bias = jnp.where(j == 0, vec_ref[4:5, :], jnp.where(j == 2, vec_ref[5:6, :], 0.0))
        value = mm(low_ref[...], mine_ref[...]) + mm(high_ref[...], other_ref[...])
        out_ref[0] = (value + bias).astype(BF16)

    weights = pl.BlockSpec((half, TILE), lambda j: (0, j))
    return run(
        body,
        (low, high, mine, other, true_vectors),
        [((3, rows, TILE), BF16)],
        (3,),
        [fixed(low.shape)] * 2 + [weights] * 2 + [pl.BlockSpec((16, TILE), lambda j: (0, at))],
        [pl.BlockSpec((1, rows, TILE), lambda j: (j, 0, 0))],
    )[0]


def head_mask(rows, side):
    lane = lax.broadcasted_iota(jnp.int32, (rows, PAIR), 1)
    return lane < PAIR // 2 if side == 0 else lane >= PAIR // 2


def attend(projected, counts):
    _, rows, width = projected[0].shape
    steps = width // PAIR

    def body(count_ref, *refs):
        *ins, out_ref, peak_ref = refs
        j = pl.program_id(0)

        def heads(q_ref, k_ref, v_ref):
            count = count_ref[0]
            key_ok = lax.broadcasted_iota(jnp.int32, (rows, rows), 1) < count
            row_ok = lax.broadcasted_iota(jnp.int32, (rows, 1), 0) < count
            queries = q_ref[0]
            out = None
            for side in (0, 1):
                chosen = head_mask(rows, side)
                scores = mm_turned(jnp.where(chosen, queries, 0), k_ref[0]) * (PAIR // 2) ** -0.5
                scores = jnp.where(key_ok, scores, masked_value)
                top = jnp.max(scores, -1, keepdims=True)
                peak = jnp.max(jnp.where(row_ok, top, masked_value))
                peak_ref[pl.ds(j * 2 + side, 1), :] = jnp.full((1, PAIR), peak)
                exponent = jnp.exp(scores - top)
                probs = exponent * (1.0 / jnp.sum(exponent, -1, keepdims=True))
                value = mm(probs.astype(BF16), v_ref[0])
                out = value if side == 0 else jnp.where(chosen, value, out)
            out_ref[...] = out.astype(BF16)

        @pl.when(j < steps)
        def _():
            heads(*ins[:3])

        @pl.when(j >= steps)
        def _():
            heads(*ins[3:])

    def part(index, at):
        return pl.BlockSpec(
            (1, rows, PAIR), lambda j: (index, 0, jnp.clip(j - at * steps, 0, steps - 1))
        )

    return run(
        body,
        (counts, *[projected[0]] * 3, *[projected[1]] * 3),
        [((rows, 2 * width), BF16), ((4 * steps, PAIR), F32)],
        (2 * steps,),
        [pl.BlockSpec(memory_space=pltpu.SMEM)]
        + [part(index, at) for at in (0, 1) for index in range(3)],
        [pl.BlockSpec((rows, PAIR), lambda j: (0, j)), fixed((4 * steps, PAIR))],
    )


def attend_back(projected, d_out, counts):
    _, rows, width = projected.shape
    steps = width // PAIR
    scale = (PAIR // 2) ** -0.5

    def body(count_ref, q_ref, k_ref, v_ref, d_ref, out_ref, sum_ref):
        key_ok = lax.broadcasted_iota(jnp.int32, (rows, rows), 0) < count_ref[0]
        queries, keys, values, grad = q_ref[0], k_ref[0], v_ref[0], d_ref[...]
        parts = [None] * 3
        for side in (0, 1):
            chosen = head_mask(rows, side)
            scores = mm_turned(jnp.where(chosen, keys, 0), queries) * scale
            scores = jnp.where(key_ok, scores, masked_value)
            exponent = jnp.exp(scores - jnp.max(scores, 0, keepdims=True))
            probs = exponent * (1.0 / jnp.sum(exponent, 0, keepdims=True))
            d_probs = mm_turned(jnp.where(chosen, values, 0), grad)
            inner = jnp.sum(probs * d_probs, 0, keepdims=True)
            d_scores = (probs * (d_probs - inner)).astype(BF16)
            new = [
                mm_rows(d_scores, keys) * scale,
                mm(d_scores, queries) * scale,
                mm(probs.astype(BF16), grad),
            ]
            parts = new if side == 0 else [jnp.where(chosen, n, p) for n, p in zip(new, parts)]
        low = [part.astype(BF16) for part in parts]
        for at in range(3):
            out_ref[at] = low[at]
        sum_ref[0:1, :] = jnp.sum(low[0].astype(F32), 0, keepdims=True)
        sum_ref[1:2, :] = jnp.sum(low[2].astype(F32), 0, keepdims=True)

    def part(index):
        return pl.BlockSpec((1, rows, PAIR), lambda j: (index, 0, j))

    columns = pl.BlockSpec((rows, PAIR), lambda j: (0, j))
    return run(
        body,
        (counts, projected, projected, projected, d_out),
        [((3, rows, width), BF16), ((8, width), F32)],
        (steps,),
        [pl.BlockSpec(memory_space=pltpu.SMEM), part(0), part(1), part(2), columns],
        [
            pl.BlockSpec((3, rows, PAIR), lambda j: (0, 0, j)),
            pl.BlockSpec((8, PAIR), lambda j: (0, j)),
        ],
    )


def second_norm(inputs, attended, weights, vectors):
    rows, width = inputs.shape
    half = width // 2

    def body(x_ref, a_ref, b_ref, wa_ref, wa2_ref, wb_ref, wb2_ref, vec_ref, mid_ref, low_ref, high_ref, lowt_ref, hight_ref):
        first, second = a_ref[...], b_ref[...]
        branch = jnp.concatenate(
            [
                mm_turned(first, wa_ref[...]) + mm_turned(second, wb_ref[...]),
                mm_turned(first, wa2_ref[...]) + mm_turned(second, wb2_ref[...]),
            ],
            1,
        )
        middle = x_ref[...].astype(F32) + branch + vec_ref[6:7, :]
        mid_ref[...] = middle
        unit, _ = normalized(middle)
        normed = (unit * vec_ref[2:3, :] + vec_ref[3:4, :]).astype(BF16)
        low_ref[...] = normed[:, :half]
        high_ref[...] = normed[:, half:]
        lowt_ref[...] = normed[:, :half].T
        hight_ref[...] = normed[:, half:].T

    block = pl.BlockSpec((half, TILE), lambda j: (0, 0))
    return run(
        body,
        (inputs, attended, attended, *weights[0], *weights[1], vectors),
        [((rows, width), F32)] + [((rows, half), BF16)] * 2 + [((half, rows), BF16)] * 2,
        (1,),
        [fixed(inputs.shape)]
        + [pl.BlockSpec((rows, TILE), lambda j, at=at: (0, at)) for at in (0, 1)]
        + [block] * 4
        + [fixed(vectors.shape)],
        [fixed((rows, width))] + [fixed((rows, half))] * 2 + [fixed((half, rows))] * 2,
    )


def expand(at, low, high, mine, other, true_vectors):
    rows, half = low.shape
    count = mine.shape[1] - TILE
    per_row = true_vectors.shape[1] // TILE
    first_row = 8 + at * count // true_vectors.shape[1]

    def body(low_ref, high_ref, mine_ref, other_ref, vec_ref, out_ref, slope_ref):
        row = first_row + pl.program_id(0) // per_row
        pre = mm(low_ref[...], mine_ref[...]) + mm(high_ref[...], other_ref[...])
        pre = pre + vec_ref[pl.ds(row, 1), :]
        below = 0.5 * (1.0 + lax.erf(pre * HALF_ROOT))
        out_ref[...] = (pre * below).astype(BF16)
        slope = below + pre * (DENSITY * jnp.exp(-0.5 * pre * pre))
        slope_ref[...] = slope.astype(BF16)

    weights = pl.BlockSpec((half, TILE), lambda j: (0, j + 1))
    columns = pl.BlockSpec((rows, TILE), lambda j: (0, j))
    return run(
        body,
        (low, high, mine, other, true_vectors),
        [((rows, count), BF16)] * 2,
        (count // TILE,),
        [fixed(low.shape)] * 2
        + [weights] * 2
        + [pl.BlockSpec((16, TILE), lambda j: (0, j % per_row))],
        [columns, columns],
    )


def expand_back(low, high, first, second, slopes):
    rows, half = low.shape
    count = slopes[0].shape[1]
    steps = count // TILE

    def body(
        low_ref, high_ref, wa_ref, wa2_ref, wb_ref, wb2_ref, sa_ref, sb_ref, out_ref, sum_ref
    ):
        def part(mine_ref, other_ref, slope_ref):
            value = mm(low_ref[...], mine_ref[...]) + mm(high_ref[...], other_ref[...])
            value = (value * slope_ref[...].astype(F32)).astype(BF16)
            out_ref[...] = value
            sum_ref[...] = jnp.sum(value.astype(F32), 0, keepdims=True)

        @pl.when(pl.program_id(0) < steps)
        def _():
            part(wa_ref, wa2_ref, sa_ref)

        @pl.when(pl.program_id(0) >= steps)
        def _():
            part(wb_ref, wb2_ref, sb_ref)

    def before(shape):
        return pl.BlockSpec(shape, lambda j: (0, jnp.minimum(j, steps - 1)))

    def behind(shape):
        return pl.BlockSpec(shape, lambda j: (0, jnp.maximum(j - steps, 0)))

    return run(
        body,
        (low, high, *first, *second, *slopes),
        [((rows, 2 * count), BF16), ((1, 2 * count), F32)],
        (2 * steps,),
        [fixed(low.shape)] * 2
        + [before((half, TILE))] * 2
        + [behind((half, TILE))] * 2
        + [before((rows, TILE)), behind((rows, TILE))],
        [pl.BlockSpec((rows, TILE), lambda j: (0, j)), pl.BlockSpec((1, TILE), lambda j: (0, j))],
    )


def contract_first(d_pre, mine, other):
    rows, count = d_pre.shape
    half = mine.shape[0]
    count = count // 2

    def body(d_ref, mine_ref, other_ref, out_ref):
        @pl.when(pl.program_id(0) == 0)
        def _():
            out_ref[...] = jnp.zeros_like(out_ref)

        out_ref[:, :half] += mm_turned(d_ref[...], mine_ref[...])
        out_ref[:, half:] += mm_turned(d_ref[...], other_ref[...])

    weights = pl.BlockSpec((half, TILE), lambda j: (0, j + 1))
    return run(
        body,
        (d_pre, mine, other),
        [((rows, 2 * half), F32)],
        (count // TILE,),
        [pl.BlockSpec((rows, TILE), lambda j: (0, j)), weights, weights],
        [fixed((rows, 2 * half))],
    )[0]


def contract_second(d_pre, weights, partial_sum, middle, d_result, vectors):
    rows, count = d_pre.shape
    half = weights[0][0].shape[0]
    width = 2 * half
    steps = count // 2 // TILE

    def body(
        d_ref, mine_ref, other_ref, wa_ref, wa2_ref, wb_ref, wb2_ref, sum_ref, mid_ref, res_ref,
        vec_ref, dm_ref, low_ref, high_ref, outa_ref, outb_ref, grads_ref, total,
    ):
        j = pl.program_id(0)

        @pl.when(j == 0)
        def _():
            total[...] = sum_ref[...]

        total[:, :half] += mm_turned(d_ref[...], mine_ref[...])
        total[:, half:] += mm_turned(d_ref[...], other_ref[...])

        @pl.when(j == steps - 1)
        def _():
            d_values, d_gain, d_shift = norm_back(total[...], mid_ref[...], vec_ref[2:3, :])
            result_grad = res_ref[...].astype(F32)
            d_middle = result_grad + d_values
            branch = d_middle.astype(BF16)
            dm_ref[...] = d_middle
            first, second = branch[:, :half], branch[:, half:]
            low_ref[...] = first.T
            high_ref[...] = second.T
            outa_ref[...] = (mm(first, wa_ref[...]) + mm(second, wa2_ref[...])).astype(BF16)
            outb_ref[...] = (mm(first, wb_ref[...]) + mm(second, wb2_ref[...])).astype(BF16)
            grads_ref[0:1, :] = d_gain
            grads_ref[1:2, :] = d_shift
            grads_ref[2:3, :] = jnp.sum(branch.astype(F32), 0, keepdims=True)
            grads_ref[3:4, :] = jnp.sum(result_grad, 0, keepdims=True)

    tile = pl.BlockSpec((half, TILE), lambda j: (0, j + 1))
    block = pl.BlockSpec((half, TILE), lambda j: (0, 0))
    return run(
        body,
        (d_pre, *weights[1], *weights[0], *weights[1], partial_sum, middle, d_result, vectors),
        [((rows, width), F32)]
        + [((half, rows), BF16)] * 2
        + [((rows, TILE), BF16)] * 2
        + [((8, width), F32)],
        (steps,),
        [pl.BlockSpec((rows, TILE), lambda j: (0, steps + j)), tile, tile]
        + [block] * 4
        + [fixed((rows, width))] * 3
        + [fixed(vectors.shape)],
        [fixed((rows, width))]
        + [fixed((half, rows))] * 2
        + [fixed((rows, TILE))] * 2
        + [fixed((8, width))],
        [pltpu.VMEM((rows, width), F32)],
    )


def input_back_first(d_projected, mine, other):
    rows = d_projected.shape[1]
    half = mine.shape[0]

    def body(d_ref, mine_ref, other_ref, out_ref):
        @pl.when(pl.program_id(0) == 0)
        def _():
            out_ref[...] = jnp.zeros_like(out_ref)

        out_ref[:, :half] += mm_turned(d_ref[0], mine_ref[...])
        out_ref[:, half:] += mm_turned(d_ref[0], other_ref[...])

    weights = pl.BlockSpec((half, TILE), lambda j: (0, j))
    return run(
        body,
        (d_projected, mine, other),
        [((rows, 2 * half), F32)],
        (3,),
        [pl.BlockSpec((1, rows, TILE), lambda j: (j, 0, 0)), weights, weights],
        [fixed((rows, 2 * half))],
    )[0]


def input_back_second(
    d_projected, mine, other, partial_sum, inputs, d_middle, grads, head_sums, d_pre_sums, vectors, to_relative
):
    rows = d_projected.shape[1]
    half = mine.shape[0]
    width = 2 * half

    def body(
        d_ref, mine_ref, other_ref, sum_ref, x_ref, dm_ref, grads_ref, heada_ref, headb_ref, pre_ref,
        vec_ref, turn_ref, out_ref, low_ref, high_ref, total, true_rows, all_rows,
    ):
        j = pl.program_id(0)

        @pl.when(j == 0)
        def _():
            total[...] = sum_ref[...]

        total[:, :half] += mm_turned(d_ref[0], mine_ref[...])
        total[:, half:] += mm_turned(d_ref[0], other_ref[...])

        @pl.when(j == 2)
        def _():
            d_values, d_gain, d_shift = norm_back(total[...], x_ref[...].astype(F32), vec_ref[0:1, :])
            low = (dm_ref[...] + d_values).astype(BF16)
            out_ref[...] = mm_turned(low, turn_ref[...]).astype(BF16)
            true_rows[...] = jnp.zeros_like(true_rows)
            for at, ref in enumerate((heada_ref, headb_ref)):
                true_rows[0:2, at * TILE : (at + 1) * TILE] = ref[0:2, :]
            for part in range(pre_ref.shape[1] // width):
                row = 2 + part
                true_rows[row : row + 1, :] = pre_ref[:, part * width : (part + 1) * width]
            turned = sum(mm(part, turn_ref[...]) for part in pieces(true_rows[...]))
            all_rows[...] = jnp.zeros_like(all_rows)
            all_rows[0:1, :] = d_gain
            all_rows[1:2, :] = d_shift
            all_rows[2:4, :] = grads_ref[0:2, :]
            all_rows[4:6, :] = turned[0:2]
            all_rows[6:8, :] = grads_ref[2:4, :]
            all_rows[8:14, :] = turned[2:8]
            columns = all_rows[...].T
            low_ref[...] = columns[:half]
            high_ref[...] = columns[half:]

    weights = pl.BlockSpec((half, TILE), lambda j: (0, j))
    operands = (
        d_projected,
        mine,
        other,
        partial_sum,
        inputs,
        d_middle,
        grads,
        *head_sums,
        d_pre_sums,
        vectors,
        to_relative,
    )
    return run(
        body,
        operands,
        [((rows, width), BF16)] + [((half, PAIR), F32)] * 2,
        (3,),
        [pl.BlockSpec((1, rows, TILE), lambda j: (j, 0, 0)), weights, weights]
        + [fixed(operand.shape) for operand in operands[3:]],
        [fixed((rows, width))] + [fixed((half, PAIR))] * 2,
        [pltpu.VMEM((rows, width), F32), pltpu.VMEM((8, width), F32), pltpu.VMEM((PAIR, width), F32)],
    )


def finish(middle, hidden, weights, vectors, to_relative, counts):
    rows, width = middle.shape
    half = width // 2
    steps = hidden[0].shape[1] // TILE

    def body(
        count_ref, a_ref, b_ref, wa_ref, wa2_ref, wb_ref, wb2_ref, mid_ref, vec_ref, turn_ref, out_ref, total
    ):
        j = pl.program_id(0)

        @pl.when(j == 0)
        def _():
            total[...] = mid_ref[...] + vec_ref[7:8, :]

        first, second = a_ref[...], b_ref[...]
        total[:, :half] += mm_turned(first, wa_ref[...]) + mm_turned(second, wb_ref[...])
        total[:, half:] += mm_turned(first, wa2_ref[...]) + mm_turned(second, wb2_ref[...])

        @pl.when(j == steps - 1)
        def _():
            kept = lax.broadcasted_iota(jnp.int32, (rows, 1), 0) < count_ref[0]
            low = jnp.where(kept, total[...], 0.0).astype(BF16)
            out_ref[...] = mm_turned(low, turn_ref[...]).astype(BF16)

    columns = pl.BlockSpec((rows, TILE), lambda j: (0, j))
    tile = pl.BlockSpec((half, TILE), lambda j: (0, j))
    return run(
        body,
        (counts, *hidden, *weights[0], *weights[1], middle, vectors, to_relative),
        [((rows, width), BF16)],
        (steps,),
        [pl.BlockSpec(memory_space=pltpu.SMEM), columns, columns]
        + [tile] * 4
        + [fixed((rows, width)), fixed(vectors.shape), fixed(to_relative.shape)],
        [fixed((rows, width))],
        [pltpu.VMEM((rows, width), F32)],
    )[0]


def product(slowest, tiles):
    count, rows = tiles[0][0].shape
    operands, specs = [], []
    for *both, width, place in tiles:
        operands += both
        specs += [fixed((count, rows))] * 2
        shape = (1,) * (len(place) - 2) + (rows, width)
        specs += [pl.BlockSpec(shape, lambda j, place=place: place)] * 2

    def body(*refs):
        *ins, sent_ref, kept_ref = refs
        first = 0
        for at, tile in enumerate(tiles):
            left, left_other, right, right_other = (
                ref[0] if len(ref.shape) == 3 else ref[...] for ref in ins[4 * at : 4 * at + 4]
            )
            value = (mm(left, right) + mm(left_other, right_other)).astype(BF16)
            columns = slice(first, first + tile[4])
            first += tile[4]
            cut_rows(value, slowest, sent_ref, kept_ref, columns)

    out = (count // 2, sum(tile[4] for tile in tiles))
    return run(body, operands, [(out, BF16)] * 2, (1,), specs, [fixed(out)] * 2)


def cut_rows(value, slowest, sent_ref, kept_ref, columns):
    part = value.shape[0] // 2 // slowest
    for group in range(slowest):
        low = 2 * group * part
        rows = slice(group * part, (group + 1) * part)
        kept_ref[rows, columns] = value[low : low + part]
        sent_ref[rows, columns] = value[low + part : low + 2 * part]


def vector_rows_cut(slowest, mine, other):
    def body(mine_ref, other_ref, sent_ref, kept_ref):
        value = (mine_ref[...] + other_ref[...]).astype(BF16)
        cut_rows(value, slowest, sent_ref, kept_ref, slice(None))

    return run(body, (mine, other), [((mine.shape[0] // 2, mine.shape[1]), BF16)] * 2)


def product_wide(slowest, first, width, left, left_other, right, right_other):
    rows = right.shape[0]
    count = left.shape[0]

    def body(left_ref, left_other_ref, right_ref, right_other_ref, sent_ref, kept_ref):
        value = mm(left_ref[...], right_ref[...]) + mm(left_other_ref[...], right_other_ref[...])
        cut_rows(value.astype(BF16), slowest, sent_ref, kept_ref, slice(None))

    columns = pl.BlockSpec((rows, TILE), lambda j: (0, first // TILE + j))
    out_columns = pl.BlockSpec((count // 2, TILE), lambda j: (0, j))
    return run(
        body,
        (left, left_other, right, right_other),
        [((count // 2, width), BF16)] * 2,
        (width // TILE,),
        [fixed(left.shape)] * 2 + [columns] * 2,
        [out_columns] * 2,
    )


def added(first, second, kind=BF16):
    return (first.astype(F32) + second.astype(F32)).astype(kind)


def halved(pairs, joined):
    half = pairs[0][0].shape[0] // 2
    widths = [mine.shape[1] for mine, _ in pairs]
    if half % 16:
        totals = [added(*pair) for pair in pairs]
        if joined:
            totals = [jnp.concatenate(totals, 1)]
        return [(total[half:], total[:half]) for total in totals]

    def body(*refs):
        ins, outs = refs[: 2 * len(pairs)], refs[2 * len(pairs) :]
        for at in range(len(pairs)):
            mine, got = ins[2 * at], ins[2 * at + 1]
            sent_ref, kept_ref = outs[:2] if joined else outs[2 * at : 2 * at + 2]
            first = sum(widths[:at]) if joined else 0
            columns = slice(first, first + widths[at])
            sent_ref[:, columns] = added(mine[half:, :], got[half:, :])
            kept_ref[:, columns] = added(mine[:half, :], got[:half, :])

    out_widths = [sum(widths)] if joined else widths
    outs = [((half, width), BF16) for width in out_widths for _ in range(2)]
    outs = run(body, [v for pair in pairs for v in pair], outs)
    return [tuple(outs[at : at + 2]) for at in range(0, len(outs), 2)]


def joined(places, middle, count, mine, got):
    wide = mine[0].shape[-1] if len(mine) == 1 else sum(value.shape[-1] for value in mine)
    parts = (slice(0, middle), slice(middle, wide))
    pairs = list(zip(places, mine, got))
    shapes = [(*value.shape[:at], 2, *value.shape[at:]) for at, value, _ in pairs]

    def widths(shape):
        if count == 1:
            return [(*shape[:-1], wide)]
        return [(*shape[:-1], part.stop - part.start) for part in parts]

    out_shapes = shapes if len(mine) == count else widths(shapes[0])
    if mine[0].shape[-2] % 16:
        both = [jnp.stack([value, come], at) for at, value, come in pairs]
        if len(mine) == count:
            return both
        if count == 1:
            rest = both[0].shape[:-1]
            return [jnp.concatenate([value.reshape(*rest, -1) for value in both], -1)]
        return [both[0][..., part] for part in parts]

    def body(*refs):
        outs = refs[2 * len(mine) :]
        for at, (place, value, _) in enumerate(pairs):
            for side in (0, 1):
                ref = refs[at + side * len(mine)]
                lead = (slice(None),) * place + (side,) + (slice(None),) * (value.ndim - 1 - place)
                if len(mine) == count:
                    outs[at][(*lead, slice(None))] = ref[...]
                elif count == 1:
                    outs[0][(*lead, parts[at])] = ref[...]
                else:
                    for out_ref, part in zip(outs, parts):
                        out_ref[(*lead, slice(None))] = ref[..., part]

    outs = [(shape, BF16) for shape in out_shapes]
    dims = mine[0].ndim - 2
    if dims < 3:
        return run(body, [*mine, *got], outs)
    def in_spec(shape):
        return pl.BlockSpec((1, 1, *shape[2:]), lambda i, j: (i, j) + (0,) * (len(shape) - 2))

    def out_spec(shape, place):
        block, at = [1, 1, *shape[3:]], lambda i, j: [i, j] + [0] * (len(shape) - 3)
        return pl.BlockSpec(
            (*block[:place], 2, *block[place:]),
            lambda i, j: (*at(i, j)[:place], 0, *at(i, j)[place:]),
        )

    return run(
        body,
        [*mine, *got],
        outs,
        mine[0].shape[:2],
        [in_spec(value.shape) for value in [*mine, *got]],
        [out_spec(shape, places[at if len(mine) == count else 0]) for at, shape in enumerate(out_shapes)],
    )


class Sum:
    def __init__(self, links, firsts):
        self.links = links
        self.left, self.pairs = [], []
        self.z_left = links.z_bits
        for parts, order in zip(firsts, links.orders):
            self.add(parts, order)

    def add(self, parts, order):
        sent, kept = parts
        self.left.append(order[1:])
        self.pairs.append((kept, self.links.exchange(sent, order[0])))

    def step(self, order):
        inner = bool(self.left[0])
        joined = not inner and len(self.pairs) > 1
        parts = order(partial(halved, joined=joined), self.pairs)
        if inner:
            bits = [left[0] for left in self.left]
            self.left = [left[1:] for left in self.left]
        else:
            bits = [self.z_left[0]]
            self.z_left = self.z_left[1:]
        self.pairs = [
            (kept, self.links.exchange(sent, bit)) for (sent, kept), bit in zip(parts, bits)
        ]

    def settle(self, order):
        self.pairs = [(kept, order.settle(got)) for kept, got in self.pairs]

    def total(self):
        return added(*self.pairs[0], F32)


class Gather:
    def __init__(self, links, shards, middle):
        self.links, self.middle = links, middle
        steps = [tuple(reversed(order)) for order in links.orders]
        steps = list(zip(*steps))
        between = len(steps) // 2 if len(shards) == 2 else 0
        z_steps = [(bit,) for bit in reversed(links.z_bits)]
        self.steps = steps[:between] + z_steps + steps[between:] + [("c", "c")]
        self.blocks = list(shards)
        self.bits = [(), ()]
        self.send()

    def send(self):
        self.got = [
            self.links.exchange(block, bit) for block, bit in zip(self.blocks, self.steps[0])
        ]

    def join(self, order):
        done, *self.steps = self.steps
        bits = done * 2 if len(done) == 1 else done
        places = []
        for at, bit in enumerate(bits):
            held = sorted((*self.bits[at], bit), key=self.links.bits.index)
            self.bits[at] = tuple(held)
            places.append(held.index(bit))
        self.blocks = order(
            partial(joined, places, self.middle, len(self.steps[0])), self.blocks, self.got
        )
        if self.steps[0][0] == "c":
            self.blocks = [block.reshape(-1, block.shape[-1]) for block in self.blocks]

    def step(self, order):
        self.join(order)
        self.send()

    def settle(self, order):
        self.got = order.settle(self.got)

    def halves(self):
        return list(zip(self.blocks, self.got))


def last_update(late, last, spans, scale, moments, vector_scale, vector_moments):
    spans, vectors_at = spans
    rows, width = moments[0].shape
    count = vector_moments[0].shape[0]

    def body(*refs):
        late_kept, late_got, last_kept, last_got, scale_ref = refs[:5]
        weight_ref, mean_ref, square_ref, vscale_ref, vector_ref, vmean_ref, vsquare_ref = refs[5:12]
        outs = refs[12:]
        sums = [added(late_kept[...], late_got[...], F32), added(last_kept[...], last_got[...], F32)]
        for of_last, first, place, size in spans:
            columns = slice(place, place + size)
            mean, square, stepped = adam_step(
                weight_ref[:, columns],
                sums[of_last][:, first : first + size],
                mean_ref[:, columns],
                square_ref[:, columns],
                matrix_rate,
                weight_decay,
            )
            outs[0][:, columns] = mean
            outs[1][:, columns] = square
            outs[2][:, columns] = stepped * scale_ref[:, columns]
        grads = sums[1][:, vectors_at : vectors_at + PAIR].T[:count]
        mean, square, stepped = adam_step(
            vector_ref[...], grads, vmean_ref[...], vsquare_ref[...], vector_rate, 0.0
        )
        outs[3][...] = mean
        outs[4][...] = square
        row = lax.broadcasted_iota(jnp.int32, stepped.shape, 0)
        outs[5][...] = jnp.where(row == 4, stepped * vscale_ref[...], stepped)

    return run(
        body,
        (*late, *last, scale, *moments, vector_scale, *vector_moments),
        [((rows, width), F32)] * 3 + [(vector_moments[0].shape, F32)] * 3,
    )


def local(
    links,
    tokens,
    cotangent,
    counts,
    w_qkv,
    w_out,
    w_up,
    w_down,
    vectors,
    mean_qkv,
    mean_out,
    mean_up,
    mean_down,
    mean_vectors,
    square_qkv,
    square_out,
    square_up,
    square_down,
    square_vectors,
):
    seq_count, slot_count, model_width = tokens.shape
    rows = seq_count * slot_count
    head_width = model_width // H
    wide = w_down.shape[0]
    vector_count, shard_width = vectors.shape
    half = model_width // 2
    order = Order()

    low_qkv = w_qkv.astype(BF16)
    thirds = [low_qkv[:, at * half : (at + 1) * half] for at in range(6)]
    shard_vectors = jnp.pad(vectors.astype(BF16).T, ((0, 0), (0, PAIR - vector_count)))
    shard_qkv = jnp.concatenate([*thirds[0::2], shard_vectors, *thirds[1::2]], 1)
    low_out, low_up = w_out.astype(BF16).T, w_up.astype(BF16)
    shard_up = jnp.concatenate(
        [low_out[:, :half], low_up[:, : wide // 2], low_out[:, half:], low_up[:, wide // 2 :]], 1
    )
    shard_down = w_down.astype(BF16).T
    gather_qkv = Gather(links, [shard_qkv], 3 * half + PAIR)
    gather_down = Gather(
        links, [shard_down[:, : wide // 2], shard_down[:, wide // 2 :]], wide // 2
    )

    true_rows = (
        links.true_block()[:, None] * shard_width + jnp.arange(shard_width, dtype=jnp.int32)
    ).reshape(1, model_width)
    to_relative = (
        lax.broadcasted_iota(jnp.int32, (model_width, model_width), 0) == true_rows
    ).astype(BF16)
    keep_rows = lax.broadcasted_iota(jnp.int32, (rows, 1), 0) < counts[0]
    d_result = jnp.where(keep_rows, cotangent.reshape(rows, model_width), 0).astype(BF16)
    inputs = mm(tokens.reshape(rows, model_width), to_relative).astype(BF16)
    d_result_turned = mm(d_result, to_relative).astype(BF16)
    d_columns = lax.dot_general(
        to_relative, d_result, (((0,), (1,)), ((), ())), preferred_element_type=F32
    ).astype(BF16)

    def longer(gather, count):
        while len(gather.steps) > count:
            gather.step(order)

    inputs, d_result_turned, d_columns, to_relative = order.settle(
        (inputs, d_result_turned, d_columns, to_relative)
    )
    d_low, d_high = d_result_turned[:, :half], d_result_turned[:, half:]
    longer(gather_qkv, 5)
    gather_qkv.step(order)
    gather_down.settle(order)
    d_other = order.settle(links.exchange(d_columns[half:], "c"))
    d_mine = d_columns[:half]
    gather_qkv.step(order)
    gather_up = Gather(
        links, [order(lambda values: values + 0, shard_up)], half + wide // 2
    )
    gather_qkv.step(order)
    longer(gather_up, 5)
    gather_up.step(order)
    gather_qkv.step(order)
    gather_up.step(order)
    longer(gather_down, 5)
    gather_down.step(order)
    halves_qkv = gather_qkv.halves()
    normed_low, normed_high, normed_mine, normed_send, vector_rows, true_vectors = order(
        first_norm, inputs, *halves_qkv[0], to_relative
    )
    normed_other = links.exchange(normed_send, "c")
    projected = [
        order(partial(project, at), normed_low, normed_high, *halves_qkv[at], true_vectors)
        for at in (0, 1)
    ]
    normed_other = order.settle(normed_other)
    gather_up.step(order)
    shared, peak = order(attend, projected, counts)
    gather_down.step(order)
    shared_other = links.exchange(shared, "c")
    peak, peak_got = [peak], []

    def peak_send(bit):
        sent = order.settle(peak[0])
        peak_got.append(links.exchange(sent, bit))

    def peak_take():
        peak[0] = order(jnp.maximum, peak[0], peak_got.pop())

    first_bit, *more_bits = links.bits
    peak_send(first_bit)
    peak_take()
    for bit in more_bits[4:]:
        peak_send(bit)
        peak_take()
    peak_send(more_bits[0])
    gather_up.step(order)
    shared_other = order.settle(shared_other)
    peak_take()
    peak_send(more_bits[1])
    peak_take()
    peak_send(more_bits[2])
    gather_down.step(order)
    peak_take()
    peak_send(more_bits[3])
    halves_up = gather_up.halves()
    middle, normed_two_low, normed_two_high, normed_two_mine, normed_two_send = order(
        second_norm, inputs, shared, halves_up, vector_rows
    )
    peak_take()
    normed_two_other = links.exchange(normed_two_send, "c")
    hidden, slope, hidden_other = [], [], []
    for at in (0, 1):
        out, out_slope = order(
            partial(expand, at), normed_two_low, normed_two_high, *halves_up[at], true_vectors
        )
        hidden.append(out)
        slope.append(out_slope)
        hidden_other.append(links.exchange(out, "c"))
        if at == 0:
            normed_two_other = order.settle(normed_two_other)
    slowest = [1, 2 ** len(links.y_bits)]

    down_parts = [
        order(
            partial(product_wide, slowest[at], 0, wide // 2),
            d_mine,
            d_other,
            hidden[at],
            hidden_other[at],
        )
        for at in (0, 1)
    ]
    gather_down.step(order)
    sum_down = Sum(links, order.settle(down_parts))
    halves_down = gather_down.halves()
    d_pre, d_pre_sums = order(expand_back, d_low, d_high, *halves_down, slope)
    d_pre_other = links.exchange(d_pre, "c")
    partial_sum = order(contract_first, d_pre, *halves_up[0])
    result = order(finish, middle, hidden, halves_down, vector_rows, to_relative, counts)
    result_out = result.reshape(seq_count, slot_count, model_width)
    for _ in links.orders[0][1:]:
        sum_down.step(order)
    sum_up = Sum(
        links,
        [
            order(
                partial(product_wide, slowest[at], at * wide // 2, wide // 2),
                normed_two_mine,
                normed_two_other,
                d_pre,
                d_pre_other,
            )
            for at in (0, 1)
        ],
    )
    d_middle, d_branch_low, d_branch_high, d_out_one, d_out_two, grads = order(
        contract_second, d_pre, halves_up, partial_sum, middle, d_result_turned, vector_rows
    )
    d_branch_other = links.exchange(d_branch_high, "c")
    sum_down.step(order)
    d_branch_other = order.settle(d_branch_other)
    d_projected, d_projected_other, head_sums = [], [], []
    for at, d_out in enumerate((d_out_one, d_out_two)):
        out, sums = order(attend_back, projected[at], d_out, counts)
        d_projected.append(out)
        d_projected_other.append(links.exchange(out, "c"))
        head_sums.append(sums)


    def out_tile(at):
        return (d_branch_low, d_branch_other, shared, shared_other, half, (0, at))

    def qkv_tile(at, part, width, column):
        return (
            normed_mine,
            normed_other,
            d_projected[at],
            d_projected_other[at],
            width,
            (part, 0, column),
        )

    def late_product(at, tiles):
        def call(*operands):
            return product(
                slowest[at],
                [(*operands[4 * i : 4 * i + 4], *tile[4:]) for i, tile in enumerate(tiles)],
            )

        return order(call, *[operand for tile in tiles for operand in tile[:4]])

    partial_sum = order(input_back_first, d_projected[0], *halves_qkv[0])
    for _ in links.z_bits[1:]:
        sum_down.step(order)
    for _ in links.orders[0][1:]:
        sum_up.step(order)
    d_projected_other = order.settle(d_projected_other)
    quarter = half // 2
    sum_late = Sum(
        links,
        [
            late_product(at, [out_tile(at), qkv_tile(0, at, half, 0), qkv_tile(0, 2, quarter, at)])
            for at in (0, 1)
        ],
    )
    last = [
        late_product(at, [qkv_tile(1, at, half, 0), qkv_tile(1, 2, quarter, at)]) for at in (0, 1)
    ]
    sum_down.settle(order)
    sum_up.step(order)
    sum_last = Sum(links, last)
    token_grad, vectors_low, vectors_high = order(
        input_back_second,
        d_projected[1],
        *halves_qkv[1],
        partial_sum,
        inputs,
        d_middle,
        grads,
        head_sums,
        d_pre_sums,
        vector_rows,
        to_relative,
    )
    token_grad = token_grad.reshape(seq_count, slot_count, model_width)
    for _ in links.orders[0][1:]:
        sum_late.step(order)
    vectors_other = order.settle(links.exchange(vectors_high, "c"))
    sum_last.add(
        order(partial(vector_rows_cut, slowest[1]), vectors_low, vectors_other), links.orders[1]
    )
    for _ in links.z_bits[1:]:
        sum_up.step(order)
    for _ in links.orders[0][1:]:
        sum_last.step(order)
    sum_late.step(order)
    sum_up.settle(order)
    sum_last.step(order)
    for _ in links.z_bits[1:]:
        sum_late.step(order)
    head_peak = order.settle(peak[0])[:, 0]
    vectors, mean_vectors, square_vectors, mean_down, first_col = order.settle(
        (
            vectors,
            mean_vectors,
            square_vectors,
            mean_down,
            lax.axis_index(("dp", "fsdp")) * shard_width,
        )
    )
    shrink = jnp.sqrt(clip_limit / jnp.maximum(head_peak, clip_limit))
    head_cols = jnp.repeat(shrink, head_width)
    qkv_scale = jnp.concatenate([head_cols, head_cols, jnp.ones((model_width,), F32)])[None]
    col_head = (first_col + jnp.arange(shard_width, dtype=jnp.int32)) // head_width
    col_shrink = jnp.sum(
        jnp.where(
            col_head[:, None] == jnp.arange(H, dtype=jnp.int32)[None, :], shrink[None, :], 0.0
        ),
        1,
    )[None]
    for _ in links.z_bits[1:]:
        sum_last.step(order)
    sum_late.settle(order)
    spans = (
        (0, half, 0, half),
        (1, 0, half, half),
        (0, half * 3 + quarter, 2 * half, half),
        (1, half + quarter, 3 * half, half),
        (0, 2 * half, 4 * half, quarter),
        (0, 4 * half + quarter, 4 * half + quarter, quarter),
        (1, half, 5 * half, quarter),
        (1, 2 * half + quarter, 5 * half + quarter, quarter),
    )
    vectors_at = 3 * half
    late = sum_late.total()
    reduced_out = jnp.concatenate([late[:, :half], late[:, 2 * half + quarter :][:, :half]], 1).T
    reduced_up = sum_up.total()
    reduced_down = sum_down.total().T
    mean_o, square_o, new_out = adam_step(
        w_out, reduced_out, mean_out, square_out, matrix_rate, weight_decay
    )
    mean_u, square_u, new_up = adam_step(
        w_up, reduced_up, mean_up, square_up, matrix_rate, weight_decay
    )
    mean_d, square_d, new_down = adam_step(
        w_down, reduced_down, mean_down, square_down, matrix_rate, weight_decay
    )
    if shard_width % 8 == 0:
        mean_q, square_q, new_qkv, mean_v, square_v, new_vectors = last_update(
            sum_late.pairs[0],
            sum_last.pairs[0],
            (spans, vectors_at),
            qkv_scale,
            (w_qkv, mean_qkv, square_qkv),
            col_shrink,
            (vectors, mean_vectors, square_vectors),
        )
    else:
        sums = (late, sum_last.total())
        reduced_qkv = jnp.concatenate(
            [sums[which][:, first : first + size] for which, first, _, size in spans], 1
        )
        mean_q, square_q, stepped_qkv = adam_step(
            w_qkv, reduced_qkv, mean_qkv, square_qkv, matrix_rate, weight_decay
        )
        new_qkv = stepped_qkv * qkv_scale
        reduced_vectors = sums[1][:, vectors_at : vectors_at + vector_count].T
        mean_v, square_v, stepped_vectors = adam_step(
            vectors, reduced_vectors, mean_vectors, square_vectors, vector_rate, 0.0
        )
        row_pick = (jnp.arange(vector_count, dtype=jnp.int32) == 4)[:, None]
        new_vectors = jnp.where(row_pick, stepped_vectors * col_shrink, stepped_vectors)
    return (
        result_out,
        token_grad,
        head_peak,
        mean_q,
        square_q,
        new_qkv,
        mean_o,
        square_o,
        new_out,
        mean_u,
        square_u,
        new_up,
        mean_d,
        square_d,
        new_down,
        mean_v,
        square_v,
        new_vectors,
    )


def solution(mesh):
    links = Links(mesh.shape["dp"], mesh.shape["fsdp"])
    return jax.shard_map(
        partial(local, links),
        mesh=mesh,
        in_specs=(
            P(("dp", "fsdp"), None, None),
            P(("dp", "fsdp"), None, None),
            P(("dp", "fsdp")),
            P(("dp", "fsdp"), None),
            P(None, ("dp", "fsdp")),
            P(("dp", "fsdp"), None),
            P(None, ("dp", "fsdp")),
            P(None, ("dp", "fsdp")),
            P(("dp", "fsdp"), None),
            P(None, ("dp", "fsdp")),
            P(("dp", "fsdp"), None),
            P(None, ("dp", "fsdp")),
            P(None, ("dp", "fsdp")),
            P(("dp", "fsdp"), None),
            P(None, ("dp", "fsdp")),
            P(("dp", "fsdp"), None),
            P(None, ("dp", "fsdp")),
            P(None, ("dp", "fsdp")),
        ),
        out_specs=(
            P(("dp", "fsdp"), None, None),
            P(("dp", "fsdp"), None, None),
            P(),
            P(("dp", "fsdp"), None),
            P(("dp", "fsdp"), None),
            P(("dp", "fsdp"), None),
            P(None, ("dp", "fsdp")),
            P(None, ("dp", "fsdp")),
            P(None, ("dp", "fsdp")),
            P(("dp", "fsdp"), None),
            P(("dp", "fsdp"), None),
            P(("dp", "fsdp"), None),
            P(None, ("dp", "fsdp")),
            P(None, ("dp", "fsdp")),
            P(None, ("dp", "fsdp")),
            P(None, ("dp", "fsdp")),
            P(None, ("dp", "fsdp")),
            P(None, ("dp", "fsdp")),
        ),
        check_vma=False,
    )
```

time: 1460 us -> 301 us (0.21)
  waiting for transfers between devices: 1170 us -> 98.6 us
  blocking collectives: 114 us -> 0 us
  Pallas kernels: 0 us -> 106 us
  matrix products: 92.8 us -> 4.17 us
  starting transfers between devices: 0.5 us -> 63.2 us
  other arithmetic: 52.4 us -> 9.3 us
    reduce_scatter x2 -> x0, waiting for transfers between devices: 991 us -> none  [the longest x1 614 us: local(): lax.psum_scatter(jnp.concatenate([contract_rows(normed_low, d_projected),...]
    all_gather x4 -> x0, waiting for transfers between devices: 175 us -> none  [the longest x1 76.8 us: local(): lax.all_gather(shard_up, ('dp', 'fsdp'), axis=0, tiled=True)]
    pallas_call x0 -> x49, Pallas kernels: none -> 106 us  [run(): pl.pallas_call(body, out_shape=[jax.ShapeDtypeStruct(shape, kind) for sha...]
    ppermute x0 -> x66, waiting for transfers between devices: none -> 98.6 us  [exchange(): lax.ppermute(values, axis, [(at, at ^ 1 << place) for at in range(count)])]
    dot_general x18 -> x3, matrix products: 92.8 us -> 4.17 us  [the longest x2 2.82 us: mm(): lax.dot_general(first, second, (((1,), (0,)), ((), ())), preferred_elemen...]
    all_gather x1 -> x0, blocking collectives: 71.4 us -> none  [local(): lax.all_gather(shard_vectors, ('dp', 'fsdp'), axis=1, tiled=True)]
    ppermute x0 -> x66, starting transfers between devices: none -> 63.2 us  [exchange(): lax.ppermute(values, axis, [(at, at ^ 1 << place) for at in range(count)])]
    pmax x1 -> x0, blocking collectives: 42.2 us -> none  [local(): head_peak = lax.pmax(local_peak, ('dp', 'fsdp'))]
  transfers between devices with their start and end apart: 6 -> 66, of which waited for: 5 -> 30; matrix products, arithmetic and copies ran while one was open for 6% -> 4% of each run, Pallas kernels for 0% -> 34%
where the time goes in v1:
time: 301 us; the launch traced here: 296 us
  Pallas kernels  106 us (35%)
  waiting for transfers between devices  98.6 us (33%)
  starting transfers between devices  63.2 us (21%)
  local copies, waits for them, and re-layouts  11.7 us (4%)
  other arithmetic  9.3 us (3%)
  matrix products  4.17 us (1%)
    pallas_call x49, Pallas kernels, run(): pl.pallas_call(body, out_shape=[jax.ShapeDtypeStruct(shape, kind) for sha...  106 us
    ppermute x66, waiting for transfers between devices, exchange(): lax.ppermute(values, axis, [(at, at ^ 1 << place) for at in range(count)])  98.6 us
    ppermute x66, starting transfers between devices, exchange(): lax.ppermute(values, axis, [(at, at ^ 1 << place) for at in range(count)])  63.2 us
    unnamed x170, local copies, waits for them, and re-layouts  11 us
  transfers between devices with their start and end apart: 66, of which 30 were waited for; matrix products, arithmetic and copies ran while one was open for 4% of the time, Pallas kernels for 34%

profile of v1, /device:TPU:0, one launch (start us, length us, event | category | flops | bytes accessed | tf_op | source)
XLA Modules:
  0.0 295.6 jit_solution(17544784553023740710)
XLA Ops:
  2.7 4.1 %collective-permute-start = (bf16[32,3200]{1,0:T(8,128)(2,1)S(1)}, bf16[32,3200]{1,0:T(8,128)(2,1)S(1)}, u32[]{:S(2)}, u32[]{:S(2)}) collective-permute-start(bf16[32,3200]{1,0:T(8,128)(2,1)S(1)} %slice_dynamic-update-slice_fusion.refs_0_), channel_id=1, source_target_pairs={{0,16},{4,20},{8,24},{12,28},{16,0},{20,4},{24,8},{28,12},{1,17},{... | collective-permute-start | bytes 614408 | tf_op jit(solution)/shard_map/ppermute | solution.py:79
  13.2 1.9 fusion.6.res_ref
  19.2 9.9 %collective-permute-done.1.refs_1_ = bf16[2,32,3200]{2,1,0:T(8,128)(2,1)S(1)} collective-permute-done((bf16[2,32,3200]{2,1,0:T(8,128)(2,1)S(1)}, bf16[2,32,3200]{2,1,0:T(8,128)(2,1)S(1)}, u32[]{:S(2)}, u32[]{:S(2)}) %collective-permute-start.1) | collective-permute-done | bytes 409632 | tf_op jit(solution)/shard_map/ppermute | solution.py:79
  30.4 3.0 %collective-permute-start.9 = (bf16[32,5120]{1,0:T(8,128)(2,1)S(1)}, bf16[32,5120]{1,0:T(8,128)(2,1)S(1)}, u32[]{:S(2)}, u32[]{:S(2)}) collective-permute-start(bf16[32,5120]{1,0:T(8,128)(2,1)S(1)} %pad_maximum_fusion.refs_0_), channel_id=1, source_target_pairs={{0,16},{4,20},{8,24},{12,28},{16,0},{20,4},{24,8},{28,12},{1,17},{... | collective-permute-start | bytes 983048 | tf_op jit(solution)/shard_map/ppermute | solution.py:79
  33.4 6.6 %collective-permute-done.6.refs_3_ = bf16[2,2,32,1536]{3,2,1,0:T(8,128)(2,1)S(1)} collective-permute-done((bf16[2,2,32,1536]{3,2,1,0:T(8,128)(2,1)S(1)}, bf16[2,2,32,1536]{3,2,1,0:T(8,128)(2,1)S(1)}, u32[]{:S(2)}, u32[]{:S(2)}) %collective-permute-start.6) | collective-permute-done | bytes 393248 | tf_op jit(solution)/shard_map/ppermute | solution.py:79
  42.2 5.0 %collective-permute-done.9.refs_1_ = bf16[32,5120]{1,0:T(8,128)(2,1)S(1)} collective-permute-done((bf16[32,5120]{1,0:T(8,128)(2,1)S(1)}, bf16[32,5120]{1,0:T(8,128)(2,1)S(1)}, u32[]{:S(2)}, u32[]{:S(2)}) %collective-permute-start.9) | collective-permute-done | bytes 327712 | tf_op jit(solution)/shard_map/ppermute | solution.py:79
  48.0 10.8 %collective-permute-done.8.refs_3_ = bf16[2,2,2,32,1536]{4,3,2,1,0:T(8,128)(2,1)S(1)} collective-permute-done((bf16[2,2,2,32,1536]{4,3,2,1,0:T(8,128)(2,1)S(1)}, bf16[2,2,2,32,1536]{4,3,2,1,0:T(8,128)(2,1)S(1)}, u32[]{:S(2)}, u32[]{:S(2)}) %collective-permute-start.8) | collective-permute-done | bytes 786464 | tf_op jit(solution)/shard_map/ppermute | solution.py:79
  61.0 2.0 collective-permute-done.11.refs_1_
  70.5 1.9 shard_map.330.refs_0_.refs_1_.refs_2_.q_ref.k_ref.v_ref
  72.4 1.8 shard_map.331.refs_3_.refs_4_.refs_5_.q_ref.k_ref.v_ref
  74.3 3.7 %collective-permute-done.13.refs_2_ = bf16[2,2,32,2560]{3,2,1,0:T(8,128)(2,1)S(1)} collective-permute-done((bf16[2,2,32,2560]{3,2,1,0:T(8,128)(2,1)S(1)}, bf16[2,2,32,2560]{3,2,1,0:T(8,128)(2,1)S(1)}, u32[]{:S(2)}, u32[]{:S(2)}) %collective-permute-start.13) | collective-permute-done | bytes 655392 | tf_op jit(solution)/shard_map/ppermute | solution.py:79
  80.8 9.0 %shard_map.333 = (bf16[320,1024]{1,0:T(8,128)(2,1)S(1)}, f32[16,128]{1,0:T(8,128)S(1)}) custom-call(s32[1]{0:T(128)} %copy.52.count_ref, bf16[3,320,512]{2,1,0:T(8,128)(2,1)S(1)} %shard_map.330.refs_0_.refs_1_.refs_2_.q_ref.k_ref.v_ref, bf16[3,320,512]{2,1,0:T(8,128)(2,1)S(1)} %shard_map.330.refs_0_.refs_1_.refs_2_.q_ref.k_ref.v_ref, ...), custom_call_target="tpu_custom_call" | custom-call | flops 30000001024 | bytes 1000 | tf_op jit(solution)/shard_map/pallas_call | solution.py:98
  89.9 3.4 %collective-permute-done.18.refs_1_ = bf16[2,32,4096]{2,1,0:T(8,128)(2,1)} collective-permute-done((bf16[2,32,4096]{2,1,0:T(8,128)(2,1)}, bf16[2,32,4096]{2,1,0:T(8,128)(2,1)}, u32[]{:S(2)}, u32[]{:S(2)}) %collective-permute-start.18) | collective-permute-done | bytes 524320 | tf_op jit(solution)/shard_map/ppermute | solution.py:79
  96.5 10.2 %collective-permute-done.16.refs_2_ = bf16[2,2,2,32,2560]{4,3,2,1,0:T(8,128)(2,1)S(1)} collective-permute-done((bf16[2,2,2,32,2560]{4,3,2,1,0:T(8,128)(2,1)S(1)}, bf16[2,2,2,32,2560]{4,3,2,1,0:T(8,128)(2,1)S(1)}, u32[]{:S(2)}, u32[]{:S(2)}) %collective-permute-start.16) | collective-permute-done | bytes 1310752 | tf_op jit(solution)/shard_map/ppermute | solution.py:79
  110.0 2.2 collective-permute-done.24
  112.2 2.3 collective-permute-start.25
  114.5 5.8 %collective-permute-done.26.refs_1_ = bf16[2,2,32,4096]{3,2,1,0:T(8,128)(2,1)S(1)} collective-permute-done((bf16[2,2,32,4096]{3,2,1,0:T(8,128)(2,1)S(1)}, bf16[2,2,32,4096]{3,2,1,0:T(8,128)(2,1)S(1)}, u32[]{:S(2)}, u32[]{:S(2)}) %collective-permute-start.26) | collective-permute-done | bytes 1048608 | tf_op jit(solution)/shard_map/ppermute | solution.py:79
  124.0 2.4 collective-permute-start.27
  130.0 3.5 %shard_map.338 = (bf16[320,2048]{1,0:T(8,128)(2,1)S(1)}, bf16[320,2048]{1,0:T(8,128)(2,1)S(1)}) custom-call(bf16[320,512]{1,0:T(8,128)(2,1)S(1)} %get-tuple-element.506.low_ref, bf16[320,512]{1,0:T(8,128)(2,1)S(1)} %get-tuple-element.507.high_ref, bf16[512,2560]{1,0:T(8,128)(2,1)S(1)} %bitcast.44, ...), custom_call_target="tpu_custom_call" | custom-call | flops 30000001024 | bytes 1000 | tf_op jit(solution)/shard_map/pallas_call | solution.py:98
  134.1 3.5 %shard_map.339 = (bf16[320,2048]{1,0:T(8,128)(2,1)S(1)}, bf16[320,2048]{1,0:T(8,128)(2,1)S(1)}) custom-call(bf16[320,512]{1,0:T(8,128)(2,1)S(1)} %get-tuple-element.506.low_ref, bf16[320,512]{1,0:T(8,128)(2,1)S(1)} %get-tuple-element.507.high_ref, bf16[512,2560]{1,0:T(8,128)(2,1)S(1)} %bitcast.49, ...), custom_call_target="tpu_custom_call" | custom-call | flops 30000001024 | bytes 1000 | tf_op jit(solution)/shard_map/pallas_call | solution.py:98
  137.7 3.2 %shard_map.340 = (bf16[256,2048]{1,0:T(8,128)(2,1)S(1)}, bf16[256,2048]{1,0:T(8,128)(2,1)S(1)}) custom-call(bf16[512,320]{1,0:T(8,128)(2,1)S(1)} %get-tuple-element.519.left_ref, bf16[512,320]{1,0:T(8,128)(2,1)S(1)} %copy-done.39, bf16[320,2048]{1,0:T(8,128)(2,1)S(1)} %get-tuple-element.549.right_ref.a_ref, ...), custom_call_target="tpu_custom_call" | custom-call | flops 30000001024 | bytes 1000 | tf_op jit(solution)/shard_map/pallas_call | solution.py:98
  142.9 3.2 %shard_map.341 = (bf16[256,2048]{1,0:T(8,128)(2,1)S(1)}, bf16[256,2048]{1,0:T(8,128)(2,1)S(1)}) custom-call(bf16[512,320]{1,0:T(8,128)(2,1)S(1)} %get-tuple-element.519.left_ref, bf16[512,320]{1,0:T(8,128)(2,1)S(1)} %copy-done.39, bf16[320,2048]{1,0:T(8,128)(2,1)S(1)} %get-tuple-element.550.right_ref.b_ref, ...), custom_call_target="tpu_custom_call" | custom-call | flops 30000001024 | bytes 1000 | tf_op jit(solution)/shard_map/pallas_call | solution.py:98
  148.0 4.3 %shard_map.342 = (bf16[2,2,2,2,32,2048]{5,4,3,2,1,0:T(8,128)(2,1)S(1)}, bf16[2,2,2,2,32,2048]{5,4,3,2,1,0:T(8,128)(2,1)}) custom-call(bf16[2,2,2,32,2048]{4,3,2,1,0:T(8,128)(2,1)} %get-tuple-element.525.refs_0_, bf16[2,2,2,32,2048]{4,3,2,1,0:T(8,128)(2,1)} %get-tuple-element.526.refs_1_, bf16[2,2,2,32,2048]{4,3,2,1,0:T(8,128)(2,1)} %collective-permute-done.29.refs_2_, ...), custom_call_target="tpu_custom_call" | custom-call | flops 30000001024 | bytes 1000 | tf_op jit(solution)/shard_map/pallas_call | solution.py:98
  154.2 5.1 %collective-permute-done.33.wa2_ref = bf16[512,2048]{1,0:T(8,128)(2,1)} collective-permute-done((bf16[512,2048]{1,0:T(8,128)(2,1)S(1)}, bf16[512,2048]{1,0:T(8,128)(2,1)}, u32[]{:S(2)}, u32[]{:S(2)}) %collective-permute-start.33) | collective-permute-done | bytes 2097184 | tf_op jit(solution)/shard_map/ppermute | solution.py:79
  162.6 8.2 %shard_map.343 = (bf16[320,4096]{1,0:T(8,128)(2,1)S(1)}, f32[1,4096]{1,0:T(1,128)S(1)}) custom-call(bf16[320,512]{1,0:T(8,128)(2,1)S(1)} %get-tuple-element.535.low_ref, bf16[320,512]{1,0:T(8,128)(2,1)S(1)} %get-tuple-element.536.high_ref, bf16[512,2048]{1,0:T(8,128)(2,1)S(1)} %bitcast.53, bf16[512,2048]{1,0:T(8,128)(2,1)} %collective-permute-done.33.wa2_ref, ...), custom_call_target="tpu_custom_call" | custom-call | flops 30000001024 | bytes 1000 | tf_op jit(solution)/shard_map/pallas_call | solution.py:98
  171.3 2.7 shard_map.344.sum_ref
  174.1 8.1 %shard_map.345 = bf16[320,1024]{1,0:T(8,128)(2,1)} custom-call(s32[1]{0:T(128)} %copy.52.count_ref, bf16[320,2048]{1,0:T(8,128)(2,1)S(1)} %copy-done.25, bf16[320,2048]{1,0:T(8,128)(2,1)S(1)} %copy-done.27, bf16[512,2048]{1,0:T(8,128)(2,1)S(1)} %bitcast.54, bf16[512,2048]{1,0:T(8,128)(2,1)} %collective-permute-done.33.wa2_ref, ...), custom_call_target="tpu_custom_call" | custom-call | flops 30000001024 | bytes 1000 | tf_op jit(solution)/shard_map/pallas_call | solution.py:98
  183.9 3.8 %shard_map.347 = (bf16[256,2048]{1,0:T(8,128)(2,1)}, bf16[256,2048]{1,0:T(8,128)(2,1)S(1)}) custom-call(bf16[512,320]{1,0:T(8,128)(2,1)S(1)} %get-tuple-element.572.left_ref, bf16[512,320]{1,0:T(8,128)(2,1)S(1)} %copy-done.41, bf16[320,4096]{1,0:T(8,128)(2,1)S(1)} %get-tuple-element.578.d_ref.right_ref, ...), custom_call_target="tpu_custom_call" | custom-call | flops 30000001024 | bytes 1000 | tf_op jit(solution)/shard_map/pallas_call | solution.py:98
  189.2 3.9 %shard_map.348 = (bf16[256,2048]{1,0:T(8,128)(2,1)}, bf16[256,2048]{1,0:T(8,128)(2,1)S(1)}) custom-call(bf16[512,320]{1,0:T(8,128)(2,1)S(1)} %get-tuple-element.572.left_ref, bf16[512,320]{1,0:T(8,128)(2,1)S(1)} %copy-done.41, bf16[320,4096]{1,0:T(8,128)(2,1)S(1)} %get-tuple-element.578.d_ref.right_ref, ...), custom_call_target="tpu_custom_call" | custom-call | flops 30000001024 | bytes 1000 | tf_op jit(solution)/shard_map/pallas_call | solution.py:98
  194.5 4.7 %shard_map.349 = (f32[320,1024]{1,0:T(8,128)S(1)}, bf16[512,320]{1,0:T(8,128)(2,1)S(1)}, bf16[512,320]{1,0:T(8,128)(2,1)S(1)}, bf16[320,512]{1,0:T(8,128)(2,1)S(...) custom-call(bf16[320,4096]{1,0:T(8,128)(2,1)S(1)} %get-tuple-element.578.d_ref.right_ref, ...), custom_call_target="tpu_custom_call" | custom-call | flops 30000001024 | bytes 1000 | tf_op jit(solution)/shard_map/pallas_call | solution.py:98
  199.6 1.8 collective-permute-start.43
  202.2 6.2 %shard_map.351 = (bf16[3,320,512]{2,1,0:T(8,128)(2,1)S(1)}, f32[8,512]{1,0:T(8,128)S(1)}) custom-call(s32[1]{0:T(128)} %copy.52.count_ref, bf16[3,320,512]{2,1,0:T(8,128)(2,1)S(1)} %copy-done.62, bf16[3,320,512]{2,1,0:T(8,128)(2,1)S(1)} %copy-done.62, bf16[3,320,512]{2,1,0:T(8,128)(2,1)S(1)} %copy-done.62, bf16[320,512]{1,0:T(8,128)(2,1)S(1)} %get-tuple-element.602.d_ref), custom_call_target="tpu_custom_call" | custom-call | flops 30000001024 | bytes 1000 | tf_op jit(solution)/shard_map/pallas_call | solution.py:98
  208.7 6.2 %shard_map.352 = (bf16[3,320,512]{2,1,0:T(8,128)(2,1)S(1)}, f32[8,512]{1,0:T(8,128)S(1)}) custom-call(s32[1]{0:T(128)} %copy.52.count_ref, bf16[3,320,512]{2,1,0:T(8,128)(2,1)S(1)} %copy-done.60, bf16[3,320,512]{2,1,0:T(8,128)(2,1)S(1)} %copy-done.60, bf16[3,320,512]{2,1,0:T(8,128)(2,1)S(1)} %copy-done.60, bf16[320,512]{1,0:T(8,128)(2,1)S(1)} %get-tuple-element.607.d_ref), custom_call_target="tpu_custom_call" | custom-call | flops 30000001024 | bytes 1000 | tf_op jit(solution)/shard_map/pallas_call | solution.py:98
  215.2 2.3 shard_map.353.sum_ref
  219.6 2.2 shard_map.355
  223.9 2.3 shard_map.356
  234.8 1.9 collective-permute-done.44.refs_1_
  238.4 1.8 collective-permute-start.57
  240.3 5.6 %shard_map.361 = (bf16[320,1024]{1,0:T(8,128)(2,1)}, f32[512,128]{1,0:T(8,128)S(1)}, f32[512,128]{1,0:T(8,128)S(1)}) custom-call(bf16[3,320,512]{2,1,0:T(8,128)(2,1)S(1)} %get-tuple-element.682.refs_2_.refs_6_.d_ref, bf16[512,1536]{1,0:T(8,128)(2,1)S(1)} %bitcast.61, bf16[512,1536]{1,0:T(8,128)(2,1)S(1)} %copy-done.23, f32[320,1024]{1,0:T(8,128)S(1)} %shard_map.353.sum_ref, ...), custom_call_target="tpu_custom_call" | custom-call | flops 30000001024 | bytes 1000 | tf_op jit(solution)/shard_map/pallas_call | solution.py:98
  245.9 4.9 %collective-permute-done.50.refs_3_ = bf16[256,1280]{1,0:T(8,128)(2,1)S(1)} collective-permute-done((bf16[256,1280]{1,0:T(8,128)(2,1)S(1)}, bf16[256,1280]{1,0:T(8,128)(2,1)S(1)}, u32[]{:S(2)}, u32[]{:S(2)}) %collective-permute-start.50) | collective-permute-done | bytes 655392 | tf_op jit(solution)/shard_map/ppermute | solution.py:79
  256.6 2.7 collective-permute-done.54.refs_3_
  259.3 2.2 collective-permute-start.62
  261.5 4.9 %collective-permute-done.56.refs_5_ = bf16[256,128]{1,0:T(8,128)(2,1)S(1)} collective-permute-done((bf16[256,128]{1,0:T(8,128)(2,1)S(1)}, bf16[256,128]{1,0:T(8,128)(2,1)S(1)}, u32[]{:S(2)}, u32[]{:S(2)}) %collective-permute-start.56) | collective-permute-done | bytes 65568 | tf_op jit(solution)/shard_map/ppermute | solution.py:79
  272.4 2.3 collective-permute-done.61.refs_5_
  277.8 5.0 %collective-permute-done.58.refs_1_ = bf16[64,2560]{1,0:T(8,128)(2,1)S(1)} collective-permute-done((bf16[64,2560]{1,0:T(8,128)(2,1)S(1)}, bf16[64,2560]{1,0:T(8,128)(2,1)S(1)}, u32[]{:S(2)}, u32[]{:S(2)}) %collective-permute-start.58) | collective-permute-done | bytes 327712 | tf_op jit(solution)/shard_map/ppermute | solution.py:79
  284.2 2.4 multiply_subtract_fusion
  289.2 1.8 collective-permute-done.63.refs_1_
  291.9 2.0 collective-permute-done.65.refs_3_
  (342 shorter events, 93.8 us)
Async XLA Ops:
  2.7 14.8 %collective-permute-start = (bf16[32,3200]{1,0:T(8,128)(2,1)S(1)}, bf16[32,3200]{1,0:T(8,128)(2,1)S(1)}, u32[]{:S(2)}, u32[]{:S(2)}) collective-permute-start(bf16[32,3200]{1,0:T(8,128)(2,1)S(1)} %slice_dynamic-update-slice_fusion.refs_0_), channel_id=1, source_target_pairs={{0,16},{4,20},{8,24},{12,28},{16,0},{20,4},{24,8},{28,12},{1,17},{... | collective-permute-start | bytes 614408 | tf_op jit(solution)/shard_map/ppermute | solution.py:79
  7.9 11.3 %collective-permute-start.3 = (bf16[32,2048]{1,0:T(8,128)(2,1)S(1)}, bf16[32,2048]{1,0:T(8,128)(2,1)S(1)}, u32[]{:S(2)}, u32[]{:S(2)}) collective-permute-start(bf16[32,2048]{1,0:T(8,128)(2,1)S(1)} %get-tuple-element.422.refs_0_), channel_id=1, source_target_pairs={{0,1},{1,0},{2,3},{3,2},{4,5},{5,4},{6,7},{7,6},{8,9},{9,8},{10,11... | collective-permute-start | bytes 393224 | tf_op jit(solution)/shard_map/ppermute | solution.py:79
  9.5 9.7 %collective-permute-start.4 = (bf16[32,2048]{1,0:T(8,128)(2,1)S(1)}, bf16[32,2048]{1,0:T(8,128)(2,1)S(1)}, u32[]{:S(2)}, u32[]{:S(2)}) collective-permute-start(bf16[32,2048]{1,0:T(8,128)(2,1)S(1)} %get-tuple-element.423.refs_1_), channel_id=1, source_target_pairs={{0,2},{1,3},{2,0},{3,1},{4,6},{5,7},{6,4},{7,5},{8,10},{9,11},{10,... | collective-permute-start | bytes 393224 | tf_op jit(solution)/shard_map/ppermute | solution.py:79
  17.5 11.7 %collective-permute-start.1 = (bf16[2,32,3200]{2,1,0:T(8,128)(2,1)S(1)}, bf16[2,32,3200]{2,1,0:T(8,128)(2,1)S(1)}, u32[]{:S(2)}, u32[]{:S(2)}) collective-permute-start(bf16[2,32,3200]{2,1,0:T(8,128)(2,1)S(1)} %shard_map.322.refs_0_), channel_id=1, source_target_pairs={{0,8},{4,12},{8,0},{12,4},{16,24},{20,28},{24,16},{28,20},{1,9},{5... | collective-permute-start | bytes 1228808 | tf_op jit(solution)/shard_map/ppermute | solution.py:79
  29.2 11.2 %collective-permute-start.5 = (bf16[2,2,32,1664]{3,2,1,0:T(8,128)(2,1)S(1)}, bf16[2,2,32,1664]{3,2,1,0:T(8,128)(2,1)S(1)}, u32[]{:S(2)}, u32[]{:S(2)}) collective-permute-start(bf16[2,2,32,1664]{3,2,1,0:T(8,128)(2,1)S(1)} %get-tuple-element.404.refs_0_), channel_id=1, source_target_pairs={{0,1},{1,0},{2,3},{3,2},{4,5},{5,4},{6,7},{7,6},{8,9},{9,8},{10,11... | collective-permute-start | bytes 1277960 | tf_op jit(solution)/shard_map/ppermute | solution.py:79
  29.8 10.1 %collective-permute-start.6 = (bf16[2,2,32,1536]{3,2,1,0:T(8,128)(2,1)S(1)}, bf16[2,2,32,1536]{3,2,1,0:T(8,128)(2,1)S(1)}, u32[]{:S(2)}, u32[]{:S(2)}) collective-permute-start(bf16[2,2,32,1536]{3,2,1,0:T(8,128)(2,1)S(1)} %get-tuple-element.405.refs_1_), channel_id=1, source_target_pairs={{0,2},{1,3},{2,0},{3,1},{4,6},{5,7},{6,4},{7,5},{8,10},{9,11},{10,... | collective-permute-start | bytes 1179656 | tf_op jit(solution)/shard_map/ppermute | solution.py:79
  30.4 16.8 %collective-permute-start.9 = (bf16[32,5120]{1,0:T(8,128)(2,1)S(1)}, bf16[32,5120]{1,0:T(8,128)(2,1)S(1)}, u32[]{:S(2)}, u32[]{:S(2)}) collective-permute-start(bf16[32,5120]{1,0:T(8,128)(2,1)S(1)} %pad_maximum_fusion.refs_0_), channel_id=1, source_target_pairs={{0,16},{4,20},{8,24},{12,28},{16,0},{20,4},{24,8},{28,12},{1,17},{... | collective-permute-start | bytes 983048 | tf_op jit(solution)/shard_map/ppermute | solution.py:79
  40.5 19.4 %collective-permute-start.7 = (bf16[2,2,2,32,1664]{4,3,2,1,0:T(8,128)(2,1)S(1)}, bf16[2,2,2,32,1664]{4,3,2,1,0:T(8,128)(2,1)S(1)}, u32[]{:S(2)}, u32[]{:S(2)}) collective-permute-start(bf16[2,2,2,32,1664]{4,3,2,1,0:T(8,128)(2,1)S(1)} %get-tuple-element.412.refs_0_), channel_id=1, source_target_pairs={{0,2},{1,3},{2,0},{3,1},{4,6},{5,7},{6,4},{7,5},{8,10},{9,11},{10,... | collective-permute-start | bytes 2555912 | tf_op jit(solution)/shard_map/ppermute | solution.py:79
  41.1 17.6 %collective-permute-start.8 = (bf16[2,2,2,32,1536]{4,3,2,1,0:T(8,128)(2,1)S(1)}, bf16[2,2,2,32,1536]{4,3,2,1,0:T(8,128)(2,1)S(1)}, u32[]{:S(2)}, u32[]{:S(2)}) collective-permute-start(bf16[2,2,2,32,1536]{4,3,2,1,0:T(8,128)(2,1)S(1)} %get-tuple-element.413.refs_1_), channel_id=1, source_target_pairs={{0,1},{1,0},{2,3},{3,2},{4,5},{5,4},{6,7},{7,6},{8,9},{9,8},{10,11... | collective-permute-start | bytes 2359304 | tf_op jit(solution)/shard_map/ppermute | solution.py:79
  47.2 15.8 %collective-permute-start.11 = (bf16[2,32,5120]{2,1,0:T(8,128)(2,1)S(1)}, bf16[2,32,5120]{2,1,0:T(8,128)(2,1)S(1)}, u32[]{:S(2)}, u32[]{:S(2)}) collective-permute-start(bf16[2,32,5120]{2,1,0:T(8,128)(2,1)S(1)} %shard_map.325.refs_0_), channel_id=1, source_target_pairs={{0,8},{4,12},{8,0},{12,4},{16,24},{20,28},{24,16},{28,20},{1,9},{5... | collective-permute-start | bytes 1966088 | tf_op jit(solution)/shard_map/ppermute | solution.py:79
  63.1 14.9 %collective-permute-start.13 = (bf16[2,2,32,2560]{3,2,1,0:T(8,128)(2,1)S(1)}, bf16[2,2,32,2560]{3,2,1,0:T(8,128)(2,1)S(1)}, u32[]{:S(2)}, u32[]{:S(2)}) collective-permute-start(bf16[2,2,32,2560]{3,2,1,0:T(8,128)(2,1)S(1)} %get-tuple-element.447.refs_0_), channel_id=1, source_target_pairs={{0,1},{1,0},{2,3},{3,2},{4,5},{5,4},{6,7},{7,6},{8,9},{9,8},{10,11... | collective-permute-start | bytes 1966088 | tf_op jit(solution)/shard_map/ppermute | solution.py:79
  64.1 14.6 %collective-permute-start.14 = (bf16[2,2,32,2560]{3,2,1,0:T(8,128)(2,1)S(1)}, bf16[2,2,32,2560]{3,2,1,0:T(8,128)(2,1)S(1)}, u32[]{:S(2)}, u32[]{:S(2)}) collective-permute-start(bf16[2,2,32,2560]{3,2,1,0:T(8,128)(2,1)S(1)} %get-tuple-element.448.refs_1_), channel_id=1, source_target_pairs={{0,2},{1,3},{2,0},{3,1},{4,6},{5,7},{6,4},{7,5},{8,10},{9,11},{10,... | collective-permute-start | bytes 1966088 | tf_op jit(solution)/shard_map/ppermute | solution.py:79
  67.0 26.3 %collective-permute-start.18 = (bf16[2,32,4096]{2,1,0:T(8,128)(2,1)}, bf16[2,32,4096]{2,1,0:T(8,128)(2,1)}, u32[]{:S(2)}, u32[]{:S(2)}) collective-permute-start(bf16[2,32,4096]{2,1,0:T(8,128)(2,1)} %shard_map.328.refs_0_), channel_id=1, source_target_pairs={{0,16},{4,20},{8,24},{12,28},{16,0},{20,4},{24,8},{28,12},{1,17},{... | collective-permute-start | bytes 1572872 | tf_op jit(solution)/shard_map/ppermute | solution.py:79
  79.0 27.7 %collective-permute-start.16 = (bf16[2,2,2,32,2560]{4,3,2,1,0:T(8,128)(2,1)S(1)}, bf16[2,2,2,32,2560]{4,3,2,1,0:T(8,128)(2,1)S(1)}, u32[]{:S(2)}, u32[]{:S(2)}) collective-permute-start(bf16[2,2,2,32,2560]{4,3,2,1,0:T(8,128)(2,1)S(1)} %get-tuple-element.464.refs_0_), channel_id=1, source_target_pairs={{0,2},{1,3},{2,0},{3,1},{4,6},{5,7},{6,4},{7,5},{8,10},{9,11},{10,... | collective-permute-start | bytes 3932168 | tf_op jit(solution)/shard_map/ppermute | solution.py:79
  80.4 27.2 %collective-permute-start.17 = (bf16[2,2,2,32,2560]{4,3,2,1,0:T(8,128)(2,1)S(1)}, bf16[2,2,2,32,2560]{4,3,2,1,0:T(8,128)(2,1)S(1)}, u32[]{:S(2)}, u32[]{:S(2)}) collective-permute-start(bf16[2,2,2,32,2560]{4,3,2,1,0:T(8,128)(2,1)S(1)} %get-tuple-element.465.refs_1_), channel_id=1, source_target_pairs={{0,1},{1,0},{2,3},{3,2},{4,5},{5,4},{6,7},{7,6},{8,9},{9,8},{10,11... | collective-permute-start | bytes 3932168 | tf_op jit(solution)/shard_map/ppermute | solution.py:79
  94.6 13.8 %collective-permute-start.23 = (bf16[320,1024]{1,0:T(8,128)(2,1)S(1)}, bf16[320,1024]{1,0:T(8,128)(2,1)S(1)}, u32[]{:S(2)}, u32[]{:S(2)}) collective-permute-start(bf16[320,1024]{1,0:T(8,128)(2,1)S(1)} %get-tuple-element.643.a_ref.b_ref.refs_2_), channel_id=1, source_target_pairs={{0,4},{4,0},{8,12},{12,8},{16,20},{20,16},{24,28},{28,24},{1,5},{5... | collective-permute-start | bytes 1966088 | tf_op jit(solution)/shard_map/ppermute | solution.py:79
  95.1 25.2 %collective-permute-start.26 = (bf16[2,2,32,4096]{3,2,1,0:T(8,128)(2,1)S(1)}, bf16[2,2,32,4096]{3,2,1,0:T(8,128)(2,1)S(1)}, u32[]{:S(2)}, u32[]{:S(2)}) collective-permute-start(bf16[2,2,32,4096]{3,2,1,0:T(8,128)(2,1)S(1)} %shard_map.334.refs_0_), channel_id=1, source_target_pairs={{0,8},{4,12},{8,0},{12,4},{16,24},{20,28},{24,16},{28,20},{1,9},{5... | collective-permute-start | bytes 3145736 | tf_op jit(solution)/shard_map/ppermute | solution.py:79
  95.8 12.7 %collective-permute-start.22 = (f32[16,128]{1,0:T(8,128)S(1)}, f32[16,128]{1,0:T(8,128)S(1)}, u32[]{:S(2)}, u32[]{:S(2)}) collective-permute-start(f32[16,128]{1,0:T(8,128)S(1)} %max.22), channel_id=1, source_target_pairs={{0,2},{1,3},{2,0},{3,1},{4,6},{5,7},{6,4},{7,5},{8,10},{9,11},{10,... | collective-permute-start | bytes 24584 | tf_op jit(solution)/shard_map/ppermute | solution.py:79
  109.5 17.0 %collective-permute-start.20 = (bf16[512,2560]{1,0:T(8,128)(2,1)S(1)}, bf16[512,2560]{1,0:T(8,128)(2,1)S(1)}, u32[]{:S(2)}, u32[]{:S(2)}) collective-permute-start(bf16[512,2560]{1,0:T(8,128)(2,1)S(1)} %bitcast.42), channel_id=1, source_target_pairs={{0,4},{4,0},{8,12},{12,8},{16,20},{20,16},{24,28},{28,24},{1,5},{5... | collective-permute-start | bytes 7864328 | tf_op jit(solution)/shard_map/ppermute | solution.py:79
  109.5 17.0 %collective-permute-start.21 = (bf16[512,2560]{1,0:T(8,128)(2,1)S(1)}, bf16[512,2560]{1,0:T(8,128)(2,1)S(1)}, u32[]{:S(2)}, u32[]{:S(2)}) collective-permute-start(bf16[512,2560]{1,0:T(8,128)(2,1)S(1)} %bitcast.47), channel_id=1, source_target_pairs={{0,4},{4,0},{8,12},{12,8},{16,20},{20,16},{24,28},{28,24},{1,5},{5... | collective-permute-start | bytes 7864328 | tf_op jit(solution)/shard_map/ppermute | solution.py:79
  112.2 11.8 %collective-permute-start.25 = (f32[16,128]{1,0:T(8,128)S(1)}, f32[16,128]{1,0:T(8,128)S(1)}, u32[]{:S(2)}, u32[]{:S(2)}) collective-permute-start(f32[16,128]{1,0:T(8,128)S(1)} %max.24), channel_id=1, source_target_pairs={{0,8},{4,12},{8,0},{12,4},{16,24},{20,28},{24,16},{28,20},{1,9},{5... | collective-permute-start | bytes 24584 | tf_op jit(solution)/shard_map/ppermute | solution.py:79
  121.8 26.2 %collective-permute-start.29 = (bf16[2,2,2,32,2048]{4,3,2,1,0:T(8,128)(2,1)}, bf16[2,2,2,32,2048]{4,3,2,1,0:T(8,128)(2,1)}, u32[]{:S(2)}, u32[]{:S(2)}) collective-permute-start(bf16[2,2,2,32,2048]{4,3,2,1,0:T(8,128)(2,1)} %get-tuple-element.525.refs_0_), channel_id=1, source_target_pairs={{0,2},{1,3},{2,0},{3,1},{4,6},{5,7},{6,4},{7,5},{8,10},{9,11},{10,... | collective-permute-start | bytes 3145736 | tf_op jit(solution)/shard_map/ppermute | solution.py:79
  122.5 25.5 %collective-permute-start.30 = (bf16[2,2,2,32,2048]{4,3,2,1,0:T(8,128)(2,1)}, bf16[2,2,2,32,2048]{4,3,2,1,0:T(8,128)(2,1)}, u32[]{:S(2)}, u32[]{:S(2)}) collective-permute-start(bf16[2,2,2,32,2048]{4,3,2,1,0:T(8,128)(2,1)} %get-tuple-element.526.refs_1_), channel_id=1, source_target_pairs={{0,1},{1,0},{2,3},{3,2},{4,5},{5,4},{6,7},{7,6},{8,9},{9,8},{10,11... | collective-permute-start | bytes 3145736 | tf_op jit(solution)/shard_map/ppermute | solution.py:79
  152.9 29.3 %collective-permute-start.36 = (bf16[256,2048]{1,0:T(8,128)(2,1)}, bf16[256,2048]{1,0:T(8,128)(2,1)S(1)}, u32[]{:S(2)}, u32[]{:S(2)}) collective-permute-start(bf16[256,2048]{1,0:T(8,128)(2,1)} %copy-done.28), channel_id=1, source_target_pairs={{0,2},{1,3},{2,0},{3,1},{4,6},{5,7},{6,4},{7,5},{8,10},{9,11},{10,... | collective-permute-start | bytes 3145736 | tf_op jit(solution)/shard_map/ppermute | solution.py:79
  153.5 28.7 %collective-permute-start.37 = (bf16[256,2048]{1,0:T(8,128)(2,1)}, bf16[256,2048]{1,0:T(8,128)(2,1)S(1)}, u32[]{:S(2)}, u32[]{:S(2)}) collective-permute-start(bf16[256,2048]{1,0:T(8,128)(2,1)} %copy-done.29), channel_id=1, source_target_pairs={{0,1},{1,0},{2,3},{3,2},{4,5},{5,4},{6,7},{7,6},{8,9},{9,8},{10,11... | collective-permute-start | bytes 3145736 | tf_op jit(solution)/shard_map/ppermute | solution.py:79
  170.8 13.0 %collective-permute-start.35 = (bf16[320,4096]{1,0:T(8,128)(2,1)S(1)}, bf16[320,4096]{1,0:T(8,128)(2,1)S(1)}, u32[]{:S(2)}, u32[]{:S(2)}) collective-permute-start(bf16[320,4096]{1,0:T(8,128)(2,1)S(1)} %get-tuple-element.578.d_ref.right_ref), channel_id=1, source_target_pairs={{0,4},{4,0},{8,12},{12,8},{16,20},{20,16},{24,28},{28,24},{1,5},{5... | collective-permute-start | bytes 7864328 | tf_op jit(solution)/shard_map/ppermute | solution.py:79
  182.7 16.6 %collective-permute-start.39 = (bf16[128,2048]{1,0:T(8,128)(2,1)S(1)}, bf16[128,2048]{1,0:T(8,128)(2,1)S(1)}, u32[]{:S(2)}, u32[]{:S(2)}) collective-permute-start(bf16[128,2048]{1,0:T(8,128)(2,1)S(1)} %get-tuple-element.562), channel_id=1, source_target_pairs={{0,1},{1,0},{2,3},{3,2},{4,5},{5,4},{6,7},{7,6},{8,9},{9,8},{10,11... | collective-permute-start | bytes 1572872 | tf_op jit(solution)/shard_map/ppermute | solution.py:79
  183.4 16.0 %collective-permute-start.40 = (bf16[128,2048]{1,0:T(8,128)(2,1)S(1)}, bf16[128,2048]{1,0:T(8,128)(2,1)S(1)}, u32[]{:S(2)}, u32[]{:S(2)}) collective-permute-start(bf16[128,2048]{1,0:T(8,128)(2,1)S(1)} %get-tuple-element.564), channel_id=1, source_target_pairs={{0,2},{1,3},{2,0},{3,1},{4,6},{5,7},{6,4},{7,5},{8,10},{9,11},{10,... | collective-permute-start | bytes 1572872 | tf_op jit(solution)/shard_map/ppermute | solution.py:79
  187.7 32.0 %collective-permute-start.41 = (bf16[256,2048]{1,0:T(8,128)(2,1)}, bf16[256,2048]{1,0:T(8,128)(2,1)}, u32[]{:S(2)}, u32[]{:S(2)}) collective-permute-start(bf16[256,2048]{1,0:T(8,128)(2,1)} %get-tuple-element.570), channel_id=1, source_target_pairs={{0,2},{1,3},{2,0},{3,1},{4,6},{5,7},{6,4},{7,5},{8,10},{9,11},{10,... | collective-permute-start | bytes 3145736 | tf_op jit(solution)/shard_map/ppermute | solution.py:79
  193.1 26.4 %collective-permute-start.42 = (bf16[256,2048]{1,0:T(8,128)(2,1)}, bf16[256,2048]{1,0:T(8,128)(2,1)}, u32[]{:S(2)}, u32[]{:S(2)}) collective-permute-start(bf16[256,2048]{1,0:T(8,128)(2,1)} %get-tuple-element.576), channel_id=1, source_target_pairs={{0,1},{1,0},{2,3},{3,2},{4,5},{5,4},{6,7},{7,6},{8,9},{9,8},{10,11... | collective-permute-start | bytes 3145736 | tf_op jit(solution)/shard_map/ppermute | solution.py:79
  199.6 17.9 %collective-permute-start.43 = (bf16[64,4096]{1,0:T(8,128)(2,1)S(1)}, bf16[64,4096]{1,0:T(8,128)(2,1)S(1)}, u32[]{:S(2)}, u32[]{:S(2)}) collective-permute-start(bf16[64,4096]{1,0:T(8,128)(2,1)S(1)} %get-tuple-element.597), channel_id=1, source_target_pairs={{0,8},{4,12},{8,0},{12,4},{16,24},{20,28},{24,16},{28,20},{1,9},{5... | collective-permute-start | bytes 1572872 | tf_op jit(solution)/shard_map/ppermute | solution.py:79
  208.4 15.5 %collective-permute-start.47 = (bf16[3,320,512]{2,1,0:T(8,128)(2,1)S(1)}, bf16[3,320,512]{2,1,0:T(8,128)(2,1)S(1)}, u32[]{:S(2)}, u32[]{:S(2)}) collective-permute-start(bf16[3,320,512]{2,1,0:T(8,128)(2,1)S(1)} %get-tuple-element.651.d_ref.refs_6_.refs_10_), channel_id=1, source_target_pairs={{0,4},{4,0},{8,12},{12,8},{16,20},{20,16},{24,28},{28,24},{1,5},{5... | collective-permute-start | bytes 2949128 | tf_op jit(solution)/shard_map/ppermute | solution.py:79
  214.8 9.0 %collective-permute-start.48 = (bf16[3,320,512]{2,1,0:T(8,128)(2,1)S(1)}, bf16[3,320,512]{2,1,0:T(8,128)(2,1)S(1)}, u32[]{:S(2)}, u32[]{:S(2)}) collective-permute-start(bf16[3,320,512]{2,1,0:T(8,128)(2,1)S(1)} %get-tuple-element.682.refs_2_.refs_6_.d_ref), channel_id=1, source_target_pairs={{0,4},{4,0},{8,12},{12,8},{16,20},{20,16},{24,28},{28,24},{1,5},{5... | collective-permute-start | bytes 2949128 | tf_op jit(solution)/shard_map/ppermute | solution.py:79
  218.3 15.2 %collective-permute-start.46 = (bf16[32,4096]{1,0:T(8,128)(2,1)}, bf16[32,4096]{1,0:T(8,128)(2,1)}, u32[]{:S(2)}, u32[]{:S(2)}) collective-permute-start(bf16[32,4096]{1,0:T(8,128)(2,1)} %get-tuple-element.615), channel_id=1, source_target_pairs={{0,16},{4,20},{8,24},{12,28},{16,0},{20,4},{24,8},{28,12},{1,17},{... | collective-permute-start | bytes 786440 | tf_op jit(solution)/shard_map/ppermute | solution.py:79
  221.8 14.9 %collective-permute-start.44 = (bf16[128,2048]{1,0:T(8,128)(2,1)S(1)}, bf16[128,2048]{1,0:T(8,128)(2,1)S(1)}, u32[]{:S(2)}, u32[]{:S(2)}) collective-permute-start(bf16[128,2048]{1,0:T(8,128)(2,1)S(1)} %get-tuple-element.622), channel_id=1, source_target_pairs={{0,1},{1,0},{2,3},{3,2},{4,5},{5,4},{6,7},{7,6},{8,9},{9,8},{10,11... | collective-permute-start | bytes 1572872 | tf_op jit(solution)/shard_map/ppermute | solution.py:79
  223.3 14.9 %collective-permute-start.45 = (bf16[128,2048]{1,0:T(8,128)(2,1)S(1)}, bf16[128,2048]{1,0:T(8,128)(2,1)S(1)}, u32[]{:S(2)}, u32[]{:S(2)}) collective-permute-start(bf16[128,2048]{1,0:T(8,128)(2,1)S(1)} %get-tuple-element.624), channel_id=1, source_target_pairs={{0,2},{1,3},{2,0},{3,1},{4,6},{5,7},{6,4},{7,5},{8,10},{9,11},{10,... | collective-permute-start | bytes 1572872 | tf_op jit(solution)/shard_map/ppermute | solution.py:79
  226.2 26.1 %collective-permute-start.49 = (bf16[256,1280]{1,0:T(8,128)(2,1)}, bf16[256,1280]{1,0:T(8,128)(2,1)}, u32[]{:S(2)}, u32[]{:S(2)}) collective-permute-start(bf16[256,1280]{1,0:T(8,128)(2,1)} %get-tuple-element.639), channel_id=1, source_target_pairs={{0,2},{1,3},{2,0},{3,1},{4,6},{5,7},{6,4},{7,5},{8,10},{9,11},{10,... | collective-permute-start | bytes 1966088 | tf_op jit(solution)/shard_map/ppermute | solution.py:79
  229.3 21.5 %collective-permute-start.50 = (bf16[256,1280]{1,0:T(8,128)(2,1)S(1)}, bf16[256,1280]{1,0:T(8,128)(2,1)S(1)}, u32[]{:S(2)}, u32[]{:S(2)}) collective-permute-start(bf16[256,1280]{1,0:T(8,128)(2,1)S(1)} %get-tuple-element.653), channel_id=1, source_target_pairs={{0,1},{1,0},{2,3},{3,2},{4,5},{5,4},{6,7},{7,6},{8,9},{9,8},{10,11... | collective-permute-start | bytes 1966088 | tf_op jit(solution)/shard_map/ppermute | solution.py:79
  233.5 25.7 %collective-permute-start.54 = (bf16[256,768]{1,0:T(8,128)(2,1)}, bf16[256,768]{1,0:T(8,128)(2,1)}, u32[]{:S(2)}, u32[]{:S(2)}) collective-permute-start(bf16[256,768]{1,0:T(8,128)(2,1)} %get-tuple-element.673), channel_id=1, source_target_pairs={{0,1},{1,0},{2,3},{3,2},{4,5},{5,4},{6,7},{7,6},{8,9},{9,8},{10,11... | collective-permute-start | bytes 1179656 | tf_op jit(solution)/shard_map/ppermute | solution.py:79
  236.7 24.8 %collective-permute-start.53 = (bf16[256,768]{1,0:T(8,128)(2,1)}, bf16[256,768]{1,0:T(8,128)(2,1)}, u32[]{:S(2)}, u32[]{:S(2)}) collective-permute-start(bf16[256,768]{1,0:T(8,128)(2,1)} %get-tuple-element.663), channel_id=1, source_target_pairs={{0,2},{1,3},{2,0},{3,1},{4,6},{5,7},{6,4},{7,5},{8,10},{9,11},{10,... | collective-permute-start | bytes 1179656 | tf_op jit(solution)/shard_map/ppermute | solution.py:79
  238.4 16.4 %collective-permute-start.57 = (bf16[64,4096]{1,0:T(8,128)(2,1)S(1)}, bf16[64,4096]{1,0:T(8,128)(2,1)S(1)}, u32[]{:S(2)}, u32[]{:S(2)}) collective-permute-start(bf16[64,4096]{1,0:T(8,128)(2,1)S(1)} %get-tuple-element.680), channel_id=1, source_target_pairs={{0,8},{4,12},{8,0},{12,4},{16,24},{20,28},{24,16},{28,20},{1,9},{5... | collective-permute-start | bytes 1572872 | tf_op jit(solution)/shard_map/ppermute | solution.py:79
  253.7 15.5 %collective-permute-start.51 = (bf16[128,1280]{1,0:T(8,128)(2,1)S(1)}, bf16[128,1280]{1,0:T(8,128)(2,1)S(1)}, u32[]{:S(2)}, u32[]{:S(2)}) collective-permute-start(bf16[128,1280]{1,0:T(8,128)(2,1)S(1)} %get-tuple-element.702), channel_id=1, source_target_pairs={{0,1},{1,0},{2,3},{3,2},{4,5},{5,4},{6,7},{7,6},{8,9},{9,8},{10,11... | collective-permute-start | bytes 983048 | tf_op jit(solution)/shard_map/ppermute | solution.py:79
  254.3 16.5 %collective-permute-start.52 = (bf16[128,1280]{1,0:T(8,128)(2,1)S(1)}, bf16[128,1280]{1,0:T(8,128)(2,1)S(1)}, u32[]{:S(2)}, u32[]{:S(2)}) collective-permute-start(bf16[128,1280]{1,0:T(8,128)(2,1)S(1)} %get-tuple-element.704), channel_id=1, source_target_pairs={{0,2},{1,3},{2,0},{3,1},{4,6},{5,7},{6,4},{7,5},{8,10},{9,11},{10,... | collective-permute-start | bytes 983048 | tf_op jit(solution)/shard_map/ppermute | solution.py:79
  254.9 11.5 %collective-permute-start.56 = (bf16[256,128]{1,0:T(8,128)(2,1)S(1)}, bf16[256,128]{1,0:T(8,128)(2,1)S(1)}, u32[]{:S(2)}, u32[]{:S(2)}) collective-permute-start(bf16[256,128]{1,0:T(8,128)(2,1)S(1)} %get-tuple-element.709), channel_id=1, source_target_pairs={{0,1},{1,0},{2,3},{3,2},{4,5},{5,4},{6,7},{7,6},{8,9},{9,8},{10,11... | collective-permute-start | bytes 196616 | tf_op jit(solution)/shard_map/ppermute | solution.py:79
  259.3 13.2 %collective-permute-start.62 = (bf16[32,4096]{1,0:T(8,128)(2,1)S(1)}, bf16[32,4096]{1,0:T(8,128)(2,1)S(1)}, u32[]{:S(2)}, u32[]{:S(2)}) collective-permute-start(bf16[32,4096]{1,0:T(8,128)(2,1)S(1)} %get-tuple-element.712), channel_id=1, source_target_pairs={{0,16},{4,20},{8,24},{12,28},{16,0},{20,4},{24,8},{28,12},{1,17},{... | collective-permute-start | bytes 786440 | tf_op jit(solution)/shard_map/ppermute | solution.py:79
  271.0 11.9 %collective-permute-start.58 = (bf16[64,2560]{1,0:T(8,128)(2,1)S(1)}, bf16[64,2560]{1,0:T(8,128)(2,1)S(1)}, u32[]{:S(2)}, u32[]{:S(2)}) collective-permute-start(bf16[64,2560]{1,0:T(8,128)(2,1)S(1)} %get-tuple-element.731), channel_id=1, source_target_pairs={{0,8},{4,12},{8,0},{12,4},{16,24},{20,28},{24,16},{28,20},{1,9},{5... | collective-permute-start | bytes 983048 | tf_op jit(solution)/shard_map/ppermute | solution.py:79
  274.9 11.8 %collective-permute-start.64 = (bf16[64,1664]{1,0:T(8,128)(2,1)S(1)}, bf16[64,1664]{1,0:T(8,128)(2,1)S(1)}, u32[]{:S(2)}, u32[]{:S(2)}) collective-permute-start(bf16[64,1664]{1,0:T(8,128)(2,1)S(1)} %get-tuple-element.739), channel_id=1, source_target_pairs={{0,8},{4,12},{8,0},{12,4},{16,24},{20,28},{24,16},{28,20},{1,9},{5... | collective-permute-start | bytes 638984 | tf_op jit(solution)/shard_map/ppermute | solution.py:79
  282.9 8.1 %collective-permute-start.63 = (bf16[32,2560]{1,0:T(8,128)(2,1)S(1)}, bf16[32,2560]{1,0:T(8,128)(2,1)S(1)}, u32[]{:S(2)}, u32[]{:S(2)}) collective-permute-start(bf16[32,2560]{1,0:T(8,128)(2,1)S(1)} %get-tuple-element.743), channel_id=1, source_target_pairs={{0,16},{4,20},{8,24},{12,28},{16,0},{20,4},{24,8},{28,12},{1,17},{... | collective-permute-start | bytes 491528 | tf_op jit(solution)/shard_map/ppermute | solution.py:79
  (100 other events, 708.3 us)
